TPU v7x, 256 devices: a whole 4x4x8 slice. The times are simulated.
256 devices in a mesh: section: 8 (over z), row: 2 (over core), col: 16 (over y, x).
Axes of the slice: x: 4, y: 4, z: 8, core: 2. Of those that a mesh axis runs over, the one named last changes fastest.
Arguments:
- in_flight: bfloat16 [8, 1024, 6144], P('section', 'row', 'col'), may hold values from -6 to 6
- injected: bfloat16 [1, 1024, 6144], P(None, 'row', 'col'), may hold values from -6 to 6
- weights: bfloat16 [8, 3, 6144, 6144], P('section', None, 'row', 'col'), may hold values from -0.078125 to 0.078125
Outputs:
- segment_out: bfloat16 [8, 1024, 6144], P('section', 'row', 'col')
All inputs are finite; a program needn't handle non-finite values.
Results may differ from a plain program's by a relative error of at most 0.0049.
Values may be sent and summed in bfloat16 or wider, within the bound.
No kernel may reach another device: no remote copies, remote signals or barrier semaphores. Data moves between devices by JAX's collectives and lax.ppermute only.
A program may use at most 128 MiB of HBM per device.

v0:
```python
import jax
import jax.numpy as jnp
from jax import lax
from jax.sharding import PartitionSpec as P

TICKS = 2


def from_behind(value, axis, steps):
    count = lax.axis_size(axis)
    first, last = (max(0, -steps), min(count, count - steps))
    return lax.ppermute(value, axis, [(source, source + steps) for source in range(first, last)])


def panel_products(acts, column_block):
    total = jnp.einsum(
        "tf,kfo->kto",
        lax.all_gather(acts, "col", axis=1, tiled=True),
        column_block,
        preferred_element_type=jnp.float32,
    )
    return (total[0], total[1], total[2])


def finish(acts, products):
    first, second, third = products
    branch = jax.nn.sigmoid(third) * jax.nn.gelu(first, approximate=True) * second
    return (acts.astype(jnp.float32) + branch).astype(jnp.bfloat16)


def body(in_flight, injected, weights):
    acts = in_flight[0]
    weight_shard = weights[0]
    first_segment = lax.axis_index("section") == 0
    output = acts
    for tick in range(TICKS):
        column_block = lax.all_gather(weight_shard, "row", axis=1, tiled=True)
        products = panel_products(acts, column_block)
        output = finish(acts, products)
        if tick + 1 < TICKS:
            passed = from_behind(output, "section", 1)
            acts = jnp.where(first_segment, injected[tick], passed)
    return output[None]


def solution(mesh):
    placed = (P("section", "row", "col"), P(None, "row", "col"), P("section", None, "row", "col"))
    return jax.shard_map(
        body, mesh=mesh, in_specs=placed, out_specs=P("section", "row", "col"), check_vma=False
    )
```

profile of v0, /device:TPU:24, one launch (start us, length us, event | category | flops | bytes accessed | tf_op | source)
XLA Modules:
  0.0 234.0 jit_solution(15691836151468640937)
XLA Ops:
  6.5 0.0 all-gather.10.cloned.1.call-start
  6.5 0.7 all-gather.10.cloned.1.call-update
  7.3 0.0 all-gather.8.cloned.1.call-start
  7.3 10.3 %copy.6 = bf16[1,3,3072,384]{2,3,1,0:T(8,128)(2,1)} copy(bf16[1,3,3072,384]{3,2,1,0:T(8,128)(2,1)} %param.5) | data formatting | bytes 14155776 | tf_op args[2]
  17.6 0.0 copy-start.1
  17.6 0.0 all-gather.8.cloned.1.call-update
  17.6 0.0 all-gather.6.cloned.1.call-start
  17.7 0.9 copy-done.1
  18.6 0.2 copy.5
  18.8 0.0 copy-start.2
  18.8 66.2 %all-gather.10.cloned.1.call-done = bf16[1,512,6144]{2,1,0:T(8,128)(2,1)} async-done(((bf16[1,512,384]{2,1,0:T(8,128)(2,1)}), bf16[1,512,6144]{2,1,0:T(8,128)(2,1)}) %all-gather.10.cloned.1.call-update) | async-done | bytes 6291472 | tf_op jit(solution)/shard_map/all_gather | solution.py:18
  84.9 33.4 %all-gather.8.cloned.1.call-done = bf16[1,3,6144,384]{2,3,1,0:T(8,128)(2,1)} async-done(((bf16[1,3,3072,384]{2,3,1,0:T(8,128)(2,1)}), bf16[1,3,6144,384]{2,3,1,0:T(8,128)(2,1)}) %all-gather.8.cloned.1.call-update) | async-done | bytes 14155792 | tf_op jit(solution)/shard_map/all_gather | solution.py:37
  118.4 12.2 %fusion.6 = f32[3,512,384]{1,2,0:T(8,128)S(1)} fusion(bf16[1,512,6144]{2,1,0:T(8,128)(2,1)} %all-gather.10.cloned.1.call-done, bf16[1,3,6144,384]{2,3,1,0:T(8,128)(2,1)} %all-gather.8.cloned.1.call-done), kind=kOutput, calls=%fused_computation.6 | convolution fusion | flops 7247757312 | bytes 22806528 | tf_op jit(solution)/shard_map/tf,kfo->kto/dot_general | solution.py:16
  130.5 0.5 fusion.26
  131.0 3.5 %collective-permute-start = (bf16[512,384]{0,1:T(8,128)(2,1)S(1)}, bf16[512,384]{0,1:T(8,128)(2,1)S(1)}, u32[]{:S(2)}, u32[]{:S(2)}) collective-permute-start(bf16[512,384]{0,1:T(8,128)(2,1)S(1)} %fusion.26), channel_id=1, source_target_pairs={{0,32},{32,64},{64,96},{96,128},{128,160},{160,192},{192,224},{1,3... | collective-permute-start | bytes 1179656 | tf_op jit(solution)/shard_map/ppermute | solution.py:12
  134.5 0.0 copy-done.2
  134.5 0.2 copy.4
  134.7 8.6 %collective-permute-done = bf16[512,384]{0,1:T(8,128)(2,1)S(1)} collective-permute-done((bf16[512,384]{0,1:T(8,128)(2,1)S(1)}, bf16[512,384]{0,1:T(8,128)(2,1)S(1)}, u32[]{:S(2)}, u32[]{:S(2)}) %collective-permute-start) | collective-permute-done | bytes 393248 | tf_op jit(solution)/shard_map/ppermute | solution.py:12
  143.3 0.8 bitcast_select_fusion
  144.1 0.0 all-gather.6.cloned.1.call-update
  144.1 0.0 copy-start
  144.1 69.9 %all-gather.6.cloned.1.call-done = bf16[512,6144]{0,1:T(8,128)(2,1)} async-done(((bf16[512,384]{0,1:T(8,128)(2,1)}), bf16[512,6144]{0,1:T(8,128)(2,1)}) %all-gather.6.cloned.1.call-update) | async-done | bytes 6291472 | tf_op jit(solution)/shard_map/all_gather | solution.py:18
  214.0 12.0 %fusion.11 = f32[3,512,384]{1,2,0:T(8,128)S(1)} fusion(bf16[1,3,6144,384]{2,3,1,0:T(8,128)(2,1)} %all-gather.8.cloned.1.call-done, bf16[512,6144]{0,1:T(8,128)(2,1)} %all-gather.6.cloned.1.call-done), kind=kOutput, calls=%fused_computation.7 | convolution fusion | flops 7247757312 | bytes 22806528 | tf_op jit(solution)/shard_map/tf,kfo->kto/dot_general | solution.py:16
  226.0 0.0 copy-done
  226.1 0.5 fusion.46
  226.5 0.9 copy.10
Async XLA Ops:
  6.5 78.4 %all-gather.10.cloned.1.call-start = ((), (), s32[]{:S(2)}) async-start(), calls=%async_computation.2 | async-start | bytes 6684672 | tf_op jit(solution)/shard_map/all_gather | solution.py:18
  7.3 111.1 %all-gather.8.cloned.1.call-start = ((), (), s32[]{:S(2)}) async-start(), calls=%async_computation.1 | async-start | bytes 21233664 | tf_op jit(solution)/shard_map/all_gather | solution.py:37
  17.6 1.0 copy-start.1
  17.6 196.4 %all-gather.6.cloned.1.call-start = ((), (), s32[]{:S(2)}) async-start(), calls=%async_computation | async-start | bytes 6684672 | tf_op jit(solution)/shard_map/all_gather | solution.py:18
  18.8 115.7 %copy-start.2 = (bf16[1,512,384]{2,1,0:T(8,128)(2,1)S(1)}, bf16[1,512,384]{2,1,0:T(8,128)(2,1)}, u32[]{:S(2)}) copy-start(bf16[1,512,384]{2,1,0:T(8,128)(2,1)} %param.4) | copy-start | bytes 1179652
  131.0 12.3 %collective-permute-start = (bf16[512,384]{0,1:T(8,128)(2,1)S(1)}, bf16[512,384]{0,1:T(8,128)(2,1)S(1)}, u32[]{:S(2)}, u32[]{:S(2)}) collective-permute-start(bf16[512,384]{0,1:T(8,128)(2,1)S(1)} %fusion.26), channel_id=1, source_target_pairs={{0,32},{32,64},{64,96},{96,128},{128,160},{160,192},{192,224},{1,3... | collective-permute-start | bytes 1179656 | tf_op jit(solution)/shard_map/ppermute | solution.py:12
  144.1 82.0 %copy-start = (bf16[512,384]{0,1:T(8,128)(2,1)S(1)}, bf16[512,384]{0,1:T(8,128)(2,1)}, u32[]{:S(2)}) copy-start(bf16[512,384]{0,1:T(8,128)(2,1)} %bitcast_select_fusion) | copy-start | bytes 1179652
Sparse Core Ops, SparseCore 0:
  9.8 75.1 all-gather.9
  86.8 31.5 all-gather.7
  144.2 69.7 all-gather.5
where the time goes:
time: 235 us; the launch traced here: 234 us
  waiting for transfers between devices  179 us (76%)
  matrix products  24.2 us (10%)
  between operations  13.2 us (6%)
  local copies, waits for them, and re-layouts  12.5 us (5%)
  starting transfers between devices  3.56 us (2%)
    all_gather x2, waiting for transfers between devices, panel_products(): lax.all_gather(acts, 'col', axis=1, tiled=True)  136 us
    all_gather x1, waiting for transfers between devices, body(): column_block = lax.all_gather(weight_shard, 'row', axis=1, tiled=True)  33.4 us
    dot_general x2, matrix products, panel_products(): jnp.einsum('tf,kfo->kto', lax.all_gather(acts, 'col', axis=1, tiled=True)...  24.2 us
    unnamed x9, local copies, waits for them, and re-layouts  11.6 us
    ppermute x1, waiting for transfers between devices, from_behind(): lax.ppermute(value, axis, [(source, source + steps) for source in range(f...  8.58 us
  transfers between devices with their start and end apart: 4, of which 4 were waited for; matrix products, arithmetic and copies ran while one was open for 5% of the time, Pallas kernels for 0%

commit v1 on v0

v1 whole, which is shorter than its diff:
```python
import functools

import jax
import jax.numpy as jnp
from jax import lax
from jax.experimental import pallas as pl
from jax.experimental.pallas import tpu as pltpu
from jax.sharding import PartitionSpec as P

TICKS = 2
SIDE = 4
PLANE = ("row", "col")


def ring_pairs(step, first):
    pairs = []
    for core in range(2):
        for col in range(SIDE * SIDE):
            y, x = divmod(col, SIDE)
            if (core == 0) == first:
                x = (x + step) % SIDE
            else:
                y = (y + step) % SIDE
            pairs.append((core * SIDE * SIDE + col, core * SIDE * SIDE + y * SIDE + x))
    return pairs


def shift(value, step, first):
    return lax.ppermute(value, PLANE, ring_pairs(step, first))


def block_ids(offsets):
    core, col = lax.axis_index("row"), lax.axis_index("col")
    y, x = col // SIDE, col % SIDE
    ids = []
    for first, second in offsets:
        along_x = jnp.where(core == 0, first, second)
        along_y = jnp.where(core == 0, second, first)
        block = (y + along_y + SIDE) % SIDE * SIDE + (x + along_x + SIDE) % SIDE
        ids += [(block // 8 + core) % 2, block % 8]
    last = lax.axis_index("section") == lax.axis_size("section") - 1
    return jnp.stack(ids + [last.astype(jnp.int32)]).astype(jnp.int32)


def products_kernel(groups, carried, final, injects, *refs):
    refs = list(refs)
    ids = refs.pop(0)
    xs = [refs.pop(0) for _ in groups]
    own, other = refs.pop(0), refs.pop(0)
    acc_in = refs.pop(0) if carried else None
    acts_in = refs.pop(0) if final else None
    inj_in = refs.pop(0) if injects else None
    out = refs.pop(0)
    x_buf, w_buf, acc, x_sem, w_sem, a_sem = refs[:6]
    rest = refs[6:]
    depth = own.shape[1] // 8
    places = [(g, i) for g, n in enumerate(groups) for i in range(n)]
    x_copies = [
        pltpu.make_async_copy(xs[g].at[i], x_buf.at[b], x_sem.at[b]) for b, (g, i) in enumerate(places)
    ]

    def w_copy(source, b):
        rows = pl.ds(pl.multiple_of(ids[2 * b + 1] * depth, depth), depth)
        return pltpu.make_async_copy(source.at[:, rows, :], w_buf.at[b], w_sem.at[b])

    def start(b):
        x_copies[b].start()

        @pl.when(ids[2 * b] == 0)
        def _():
            w_copy(own, b).start()

        @pl.when(ids[2 * b] != 0)
        def _():
            w_copy(other, b).start()

    start(0)
    start(1)
    if carried:
        acc_copy = pltpu.make_async_copy(acc_in, acc, a_sem.at[0])
        acc_copy.start()
    for b in range(2, len(places)):
        start(b)
    if final:
        acts_copy = pltpu.make_async_copy(acts_in, rest[0], a_sem.at[1])
        acts_copy.start()
    if injects:
        inj_copy = pltpu.make_async_copy(inj_in, rest[1], a_sem.at[2])
        inj_copy.start()
    for pair in range(len(places) // 2):
        for b in (2 * pair, 2 * pair + 1):
            x_copies[b].wait()
            w_copy(own, b).wait()
        x = jnp.concatenate([x_buf[2 * pair], x_buf[2 * pair + 1]], axis=1)
        if carried and pair == 0:
            acc_copy.wait()
        for k in range(3):
            w = jnp.concatenate([w_buf[2 * pair, k], w_buf[2 * pair + 1, k]], axis=0)
            part = jnp.dot(x, w, preferred_element_type=jnp.float32)
            if carried or pair > 0:
                part = acc[k] + part
            acc[k] = part
    if not final:
        out_copy = pltpu.make_async_copy(acc, out, a_sem.at[1])
        out_copy.start()
        out_copy.wait()
        return
    acts_copy.wait()
    if injects:
        inj_copy.wait()
    rows = 64

    @pl.loop(0, acc.shape[1] // rows)
    def _(i):
        at = pl.ds(pl.multiple_of(i * rows, rows), rows)
        first, second, third = acc[0, at], acc[1, at], acc[2, at]
        gate = 1.0 / (1.0 + jnp.exp(-third))
        cubic = 0.7978845608 * (first + 0.044715 * (first * first * first))
        value = rest[0][at].astype(jnp.float32) + gate * (0.5 * first * (1.0 + jnp.tanh(cubic))) * second
        value = value.astype(jnp.bfloat16)
        if injects:
            value = jnp.where(ids[2 * len(places)] != 0, rest[1][at], value)
        out[at] = value


def products(ids, groups, own, other, acc=None, acts=None, injected=None):
    tokens, width = groups[0].shape[1:]
    counts = tuple(g.shape[0] for g in groups)
    blocks = sum(counts)
    final = acts is not None
    injects = injected is not None
    operands = [ids, *groups, own, other]
    aliases = {}
    if acc is not None:
        if not final:
            aliases = {len(operands): 0}
        operands.append(acc)
    operands += [v for v in (acts, injected) if v is not None]
    scratch = [
        pltpu.VMEM((blocks, tokens, width), jnp.bfloat16),
        pltpu.VMEM((blocks, 3, width, width), jnp.bfloat16),
        pltpu.VMEM((3, tokens, width), jnp.float32),
        pltpu.SemaphoreType.DMA((blocks,)),
        pltpu.SemaphoreType.DMA((blocks,)),
        pltpu.SemaphoreType.DMA((3,)),
    ]
    scratch += [pltpu.VMEM((tokens, width), jnp.bfloat16)] * (final + injects)
    return pl.pallas_call(
        functools.partial(products_kernel, counts, acc is not None, final, injects),
        out_shape=jax.ShapeDtypeStruct((tokens, width), jnp.bfloat16)
        if final
        else jax.ShapeDtypeStruct((3, tokens, width), jnp.float32),
        in_specs=[pl.BlockSpec(memory_space=pltpu.SMEM)]
        + [pl.BlockSpec(memory_space=pl.ANY)] * (len(operands) - 1),
        out_specs=pl.BlockSpec(memory_space=pltpu.VMEM if final else pl.ANY),
        scratch_shapes=scratch,
        input_output_aliases=aliases,
        compiler_params=pltpu.CompilerParams(vmem_limit_bytes=24 * 1024 * 1024),
        cost_estimate=pl.CostEstimate(
            flops=2 * blocks * tokens * width * width * 3,
            bytes_accessed=2 * blocks * width * (tokens + 3 * width),
            transcendentals=0,
        ),
    )(*operands)


def block(acts, own, other, injected=None):
    near = [acts] + [shift(acts, step, True) for step in (1, 3, 2)]
    low, high = jnp.stack(near[:2]), jnp.stack(near[2:])
    low_at, high_at = (0, -1), (1, 2)

    def ids(*parts):
        return block_ids([(one, two) for at, two in parts for one in at])

    up_low, down_high = shift(low, 1, False), shift(high, 3, False)
    up_high, down_low = shift(high, 1, False), shift(low, 3, False)
    far_low, far_high = shift(up_low, 1, False), shift(down_high, 3, False)
    acc = products(ids((low_at, 0), (high_at, 0)), [low, high], own, other)
    acc = products(ids((low_at, -1), (high_at, 1)), [up_low, down_high], own, other, acc)
    acc = products(ids((high_at, -1), (low_at, 1)), [up_high, down_low], own, other, acc)
    return products(
        ids((low_at, 2), (high_at, 2)), [far_low, far_high], own, other, acc, acts, injected
    )


def body(in_flight, injected, weights):
    own = weights[0]
    other = lax.ppermute(own, "row", [(0, 1), (1, 0)])
    count = lax.axis_size("section")
    acts = in_flight[0]
    for tick in range(TICKS - 1):
        output = block(acts, own, other, injected[tick])
        acts = lax.ppermute(output, "section", [(s, (s + 1) % count) for s in range(count)])
    return block(acts, own, other)[None]


def solution(mesh):
    placed = (P("section", "row", "col"), P(None, "row", "col"), P("section", None, "row", "col"))
    return jax.shard_map(
        body, mesh=mesh, in_specs=placed, out_specs=P("section", "row", "col"), check_vma=False
    )
```

time: 235 us -> 122 us (0.52)
  waiting for transfers between devices: 179 us -> 51.7 us
  Pallas kernels: 0 us -> 42.6 us
  matrix products: 24.2 us -> 0 us
  starting transfers between devices: 3.56 us -> 21.8 us
  between operations: 13.2 us -> 0.39 us
  local copies, waits for them, and re-layouts: 12.5 us -> 3.36 us
    all_gather x3 -> x0, waiting for transfers between devices: 169 us -> none  [the longest x2 136 us: panel_products(): lax.all_gather(acts, 'col', axis=1, tiled=True)]
    ppermute x1 -> x20, waiting for transfers between devices: 8.58 us -> 51.7 us  [the longest x18 41.2 us: shift(): return lax.ppermute(value, PLANE, ring_pairs(step, first))]
    pallas_call x0 -> x8, Pallas kernels: none -> 42.6 us  [products(): pl.pallas_call(functools.partial(products_kernel, counts, acc is not None...]
    dot_general x2 -> x0, matrix products: 24.2 us -> none  [panel_products(): jnp.einsum('tf,kfo->kto', lax.all_gather(acts, 'col', axis=1, tiled=True)...]
    ppermute x1 -> x20, starting transfers between devices: 3.48 us -> 21.8 us  [the longest x18 19.8 us: shift(): return lax.ppermute(value, PLANE, ring_pairs(step, first))]
    unnamed x9 -> x8, local copies, waits for them, and re-layouts: 11.6 us -> 3.02 us
  transfers between devices with their start and end apart: 4 -> 20, of which waited for: 4 -> 9; matrix products, arithmetic and copies ran while one was open for 5% -> 1% of each run, Pallas kernels for 0% -> 26%
where the time goes in v1:
time: 122 us; the launch traced here: 121 us
  waiting for transfers between devices  51.7 us (42%)
  Pallas kernels  42.6 us (35%)
  starting transfers between devices  21.8 us (18%)
  local copies, waits for them, and re-layouts  3.36 us (3%)
  other arithmetic  1.36 us (1%)
    pallas_call x8, Pallas kernels, products(): pl.pallas_call(functools.partial(products_kernel, counts, acc is not None...  42.6 us
    ppermute x18, waiting for transfers between devices, shift(): return lax.ppermute(value, PLANE, ring_pairs(step, first))  41.2 us
    ppermute x18, starting transfers between devices, shift(): return lax.ppermute(value, PLANE, ring_pairs(step, first))  19.8 us
    ppermute x1, waiting for transfers between devices, body(): lax.ppermute(output, 'section', [(s, (s + 1) % count) for s in range(coun...  10.6 us
    unnamed x8, local copies, waits for them, and re-layouts  3.02 us
  transfers between devices with their start and end apart: 20, of which 9 were waited for; matrix products, arithmetic and copies ran while one was open for 1% of the time, Pallas kernels for 26%

profile of v1, /device:TPU:24, one launch (start us, length us, event | category | flops | bytes accessed | tf_op | source)
XLA Modules:
  0.0 121.3 jit_solution(3400081760904123463)
XLA Ops:
  0.0 2.8 %collective-permute-start.3 = (bf16[512,384]{1,0:T(8,128)(2,1)}, bf16[512,384]{1,0:T(8,128)(2,1)S(1)}, u32[]{:S(2)}, u32[]{:S(2)}) collective-permute-start(bf16[512,384]{1,0:T(8,128)(2,1)} %bitcast.53), channel_id=1, source_target_pairs={{0,3},{1,0},{2,1},{3,2},{4,7},{5,4},{6,5},{7,6},{8,11},{9,8},{10,9... | collective-permute-start | bytes 1179656 | tf_op jit(solution)/shard_map/ppermute | solution.py:29
  2.8 0.8 collective-permute-start.4
  3.6 0.9 collective-permute-start
  4.4 8.2 %collective-permute-done.3 = bf16[512,384]{1,0:T(8,128)(2,1)S(1)} collective-permute-done((bf16[512,384]{1,0:T(8,128)(2,1)}, bf16[512,384]{1,0:T(8,128)(2,1)S(1)}, u32[]{:S(2)}, u32[]{:S(2)}) %collective-permute-start.3) | collective-permute-done | bytes 393248 | tf_op jit(solution)/shard_map/ppermute | solution.py:29
  12.7 0.8 collective-permute-start.5
  13.5 2.9 %collective-permute-done = bf16[512,384]{1,0:T(8,128)(2,1)S(1)} collective-permute-done((bf16[512,384]{1,0:T(8,128)(2,1)}, bf16[512,384]{1,0:T(8,128)(2,1)S(1)}, u32[]{:S(2)}, u32[]{:S(2)}) %collective-permute-start) | collective-permute-done | bytes 393248 | tf_op jit(solution)/shard_map/ppermute | solution.py:29
  16.5 1.1 pad_maximum_fusion.refs_1_
  17.9 1.6 %collective-permute-start.8 = (bf16[2,512,384]{2,1,0:T(8,128)(2,1)S(1)}, bf16[2,512,384]{2,1,0:T(8,128)(2,1)}, u32[]{:S(2)}, u32[]{:S(2)}) collective-permute-start(bf16[2,512,384]{2,1,0:T(8,128)(2,1)S(1)} %pad_maximum_fusion.1.refs_2_), channel_id=1, source_target_pairs={{0,4},{1,5},{2,6},{3,7},{4,8},{5,9},{6,10},{7,11},{8,12},{9,13},{1... | collective-permute-start | bytes 2359304 | tf_op jit(solution)/shard_map/ppermute | solution.py:29
  19.4 0.4 collective-permute-start.9
  19.9 6.1 %collective-permute-done.5.refs_2_ = bf16[2,512,384]{2,1,0:T(8,128)(2,1)S(1)} collective-permute-done((bf16[2,512,384]{2,1,0:T(8,128)(2,1)S(1)}, bf16[2,512,384]{2,1,0:T(8,128)(2,1)S(1)}, u32[]{:S(2)}, u32[]{:S(2)}) %collective-permute-start.5) | collective-permute-done | bytes 786464 | tf_op jit(solution)/shard_map/ppermute | solution.py:29
  26.0 3.6 %collective-permute-done.1.refs_1_ = bf16[2,512,384]{2,1,0:T(8,128)(2,1)S(1)} collective-permute-done((bf16[2,512,384]{2,1,0:T(8,128)(2,1)S(1)}, bf16[2,512,384]{2,1,0:T(8,128)(2,1)S(1)}, u32[]{:S(2)}, u32[]{:S(2)}) %collective-permute-start.1) | collective-permute-done | bytes 786464 | tf_op jit(solution)/shard_map/ppermute | solution.py:29
  29.6 1.4 %collective-permute-start.2 = (bf16[2,512,384]{2,1,0:T(8,128)(2,1)S(1)}, bf16[2,512,384]{2,1,0:T(8,128)(2,1)}, u32[]{:S(2)}, u32[]{:S(2)}) collective-permute-start(bf16[2,512,384]{2,1,0:T(8,128)(2,1)S(1)} %collective-permute-done.1.refs_1_), channel_id=1, source_target_pairs={{0,4},{1,5},{2,6},{3,7},{4,8},{5,9},{6,10},{7,11},{8,12},{9,13},{1... | collective-permute-start | bytes 2359304 | tf_op jit(solution)/shard_map/ppermute | solution.py:29
  31.4 3.0 %copy-done = bf16[1,3,3072,384]{3,2,1,0:T(8,128)(2,1)S(1)} copy-done((bf16[1,3,3072,384]{3,2,1,0:T(8,128)(2,1)S(1)}, bf16[1,3,3072,384]{3,2,1,0:T(8,128)(2,1)}, u32[]{:S(2)}) %copy-start) | copy-done | bytes 7077912
  34.4 5.4 %shard_map.37.refs_5_ = f32[3,512,384]{2,1,0:T(8,128)S(1)} custom-call(s32[9]{0:T(128)S(1)} %stack.232.refs_0_, bf16[2,512,384]{2,1,0:T(8,128)(2,1)S(1)} %pad_maximum_fusion.refs_1_, bf16[2,512,384]{2,1,0:T(8,128)(2,1)S(1)} %pad_maximum_fusion.1.refs_2_, bf16[3,3072,384]{2,1,0:T(8,128)(2,1)S(1)} %bitcast.45, bf16[3,3072,384]{2,1,0:T(8,128)(2,1)} %collective-permute-done.7.refs_4_), custom_call_target="tpu_custom_call" | custom-call | flops 1811939328 | bytes 5111808 | tf_op jit(solution)/shard_map/pallas_call | solution.py:148
  39.9 5.2 %shard_map.38.refs_5_ = f32[3,512,384]{2,1,0:T(8,128)S(1)} custom-call(s32[9]{0:T(128)S(1)} %stack.223.refs_0_, bf16[2,512,384]{2,1,0:T(8,128)(2,1)S(1)} %collective-permute-done.1.refs_1_, bf16[2,512,384]{2,1,0:T(8,128)(2,1)S(1)} %collective-permute-done.5.refs_2_, bf16[3,3072,384]{2,1,0:T(8,128)(2,1)S(1)} %bitcast.46, ...), custom_call_target="tpu_custom_call", output_to_operand_aliasing={{}: (5, {})} | custom-call | flops 1811939328 | bytes 5111808 | tf_op jit(solution)/shard_map/pallas_call | solution.py:148
  45.1 5.2 %shard_map.39.refs_5_ = f32[3,512,384]{2,1,0:T(8,128)S(1)} custom-call(s32[9]{0:T(128)S(1)} %stack.214.refs_0_, bf16[2,512,384]{2,1,0:T(8,128)(2,1)} %collective-permute-done.8.refs_1_, bf16[2,512,384]{2,1,0:T(8,128)(2,1)} %collective-permute-done.9.refs_2_, bf16[3,3072,384]{2,1,0:T(8,128)(2,1)S(1)} %bitcast.47, ...), custom_call_target="tpu_custom_call", output_to_operand_aliasing={{}: (5, {})} | custom-call | flops 1811939328 | bytes 5111808 | tf_op jit(solution)/shard_map/pallas_call | solution.py:148
  50.4 5.1 %shard_map.40 = bf16[512,384]{1,0:T(8,128)(2,1)S(1)} custom-call(s32[9]{0:T(128)S(1)} %stack.200.refs_0_, bf16[2,512,384]{2,1,0:T(8,128)(2,1)} %collective-permute-done.2.refs_1_, bf16[2,512,384]{2,1,0:T(8,128)(2,1)} %collective-permute-done.6.refs_2_, bf16[3,3072,384]{2,1,0:T(8,128)(2,1)S(1)} %bitcast.48, ...), custom_call_target="tpu_custom_call" | custom-call | flops 1811939328 | bytes 5111808 | tf_op jit(solution)/shard_map/pallas_call | solution.py:148
  55.5 2.0 %collective-permute-start.10 = (bf16[512,384]{1,0:T(8,128)(2,1)S(1)}, bf16[512,384]{1,0:T(8,128)(2,1)S(1)}, u32[]{:S(2)}, u32[]{:S(2)}) collective-permute-start(bf16[512,384]{1,0:T(8,128)(2,1)S(1)} %shard_map.40), channel_id=1, source_target_pairs={{0,32},{32,64},{64,96},{96,128},{128,160},{160,192},{192,224},{224... | collective-permute-start | bytes 1179656 | tf_op jit(solution)/shard_map/ppermute | solution.py:193
  57.5 10.6 %collective-permute-done.10.refs_6_ = bf16[512,384]{1,0:T(8,128)(2,1)S(1)} collective-permute-done((bf16[512,384]{1,0:T(8,128)(2,1)S(1)}, bf16[512,384]{1,0:T(8,128)(2,1)S(1)}, u32[]{:S(2)}, u32[]{:S(2)}) %collective-permute-start.10) | collective-permute-done | bytes 393248 | tf_op jit(solution)/shard_map/ppermute | solution.py:193
  68.0 3.0 %collective-permute-start.14 = (bf16[512,384]{1,0:T(8,128)(2,1)S(1)}, bf16[512,384]{1,0:T(8,128)(2,1)S(1)}, u32[]{:S(2)}, u32[]{:S(2)}) collective-permute-start(bf16[512,384]{1,0:T(8,128)(2,1)S(1)} %collective-permute-done.10.refs_6_), channel_id=1, source_target_pairs={{0,3},{1,0},{2,1},{3,2},{4,7},{5,4},{6,5},{7,6},{8,11},{9,8},{10,9... | collective-permute-start | bytes 1179656 | tf_op jit(solution)/shard_map/ppermute | solution.py:29
  71.0 0.9 collective-permute-start.11
  71.8 8.6 %collective-permute-done.14 = bf16[512,384]{1,0:T(8,128)(2,1)S(1)} collective-permute-done((bf16[512,384]{1,0:T(8,128)(2,1)S(1)}, bf16[512,384]{1,0:T(8,128)(2,1)S(1)}, u32[]{:S(2)}, u32[]{:S(2)}) %collective-permute-start.14) | collective-permute-done | bytes 393248 | tf_op jit(solution)/shard_map/ppermute | solution.py:29
  80.7 3.5 %collective-permute-done.11 = bf16[512,384]{1,0:T(8,128)(2,1)S(1)} collective-permute-done((bf16[512,384]{1,0:T(8,128)(2,1)S(1)}, bf16[512,384]{1,0:T(8,128)(2,1)S(1)}, u32[]{:S(2)}, u32[]{:S(2)}) %collective-permute-start.11) | collective-permute-done | bytes 393248 | tf_op jit(solution)/shard_map/ppermute | solution.py:29
  84.3 1.9 %collective-permute-start.12 = (bf16[2,512,384]{2,1,0:T(8,128)(2,1)S(1)}, bf16[2,512,384]{2,1,0:T(8,128)(2,1)S(1)}, u32[]{:S(2)}, u32[]{:S(2)}) collective-permute-start(bf16[2,512,384]{2,1,0:T(8,128)(2,1)S(1)} %pad_maximum_fusion.2.refs_1_), channel_id=1, source_target_pairs={{0,4},{1,5},{2,6},{3,7},{4,8},{5,9},{6,10},{7,11},{8,12},{9,13},{1... | collective-permute-start | bytes 2359304 | tf_op jit(solution)/shard_map/ppermute | solution.py:29
  86.2 1.9 %collective-permute-start.19 = (bf16[2,512,384]{2,1,0:T(8,128)(2,1)S(1)}, bf16[2,512,384]{2,1,0:T(8,128)(2,1)S(1)}, u32[]{:S(2)}, u32[]{:S(2)}) collective-permute-start(bf16[2,512,384]{2,1,0:T(8,128)(2,1)S(1)} %pad_maximum_fusion.2.refs_1_), channel_id=1, source_target_pairs={{0,12},{1,13},{2,14},{3,15},{4,0},{5,1},{6,2},{7,3},{8,4},{9,5},{1... | collective-permute-start | bytes 2359304 | tf_op jit(solution)/shard_map/ppermute | solution.py:29
  88.2 5.7 %collective-permute-done.16.refs_2_ = bf16[2,512,384]{2,1,0:T(8,128)(2,1)S(1)} collective-permute-done((bf16[2,512,384]{2,1,0:T(8,128)(2,1)S(1)}, bf16[2,512,384]{2,1,0:T(8,128)(2,1)S(1)}, u32[]{:S(2)}, u32[]{:S(2)}) %collective-permute-start.16) | collective-permute-done | bytes 786464 | tf_op jit(solution)/shard_map/ppermute | solution.py:29
  93.9 2.5 %collective-permute-done.12.refs_1_ = bf16[2,512,384]{2,1,0:T(8,128)(2,1)S(1)} collective-permute-done((bf16[2,512,384]{2,1,0:T(8,128)(2,1)S(1)}, bf16[2,512,384]{2,1,0:T(8,128)(2,1)S(1)}, u32[]{:S(2)}, u32[]{:S(2)}) %collective-permute-start.12) | collective-permute-done | bytes 786464 | tf_op jit(solution)/shard_map/ppermute | solution.py:29
  96.3 3.0 %collective-permute-start.13 = (bf16[2,512,384]{2,1,0:T(8,128)(2,1)S(1)}, bf16[2,512,384]{2,1,0:T(8,128)(2,1)S(1)}, u32[]{:S(2)}, u32[]{:S(2)}) collective-permute-start(bf16[2,512,384]{2,1,0:T(8,128)(2,1)S(1)} %collective-permute-done.12.refs_1_), channel_id=1, source_target_pairs={{0,4},{1,5},{2,6},{3,7},{4,8},{5,9},{6,10},{7,11},{8,12},{9,13},{1... | collective-permute-start | bytes 2359304 | tf_op jit(solution)/shard_map/ppermute | solution.py:29
  99.3 5.2 %shard_map.41.refs_5_ = f32[3,512,384]{2,1,0:T(8,128)S(1)} custom-call(s32[9]{0:T(128)S(1)} %stack.232.refs_0_, bf16[2,512,384]{2,1,0:T(8,128)(2,1)S(1)} %pad_maximum_fusion.2.refs_1_, bf16[2,512,384]{2,1,0:T(8,128)(2,1)S(1)} %pad_maximum_fusion.3.refs_2_, bf16[3,3072,384]{2,1,0:T(8,128)(2,1)S(1)} %bitcast.49, ...), custom_call_target="tpu_custom_call" | custom-call | flops 1811939328 | bytes 5111808 | tf_op jit(solution)/shard_map/pallas_call | solution.py:148
  104.5 5.2 %shard_map.42.refs_5_ = f32[3,512,384]{2,1,0:T(8,128)S(1)} custom-call(s32[9]{0:T(128)S(1)} %stack.223.refs_0_, bf16[2,512,384]{2,1,0:T(8,128)(2,1)S(1)} %collective-permute-done.12.refs_1_, bf16[2,512,384]{2,1,0:T(8,128)(2,1)S(1)} %collective-permute-done.16.refs_2_, bf16[3,3072,384]{2,1,0:T(8,128)(2,1)S(1)} %bitcast.50, ...), custom_call_target="tpu_custom_call", output_to_operand_aliasing={{}: (5, {})} | custom-call | flops 1811939328 | bytes 5111808 | tf_op jit(solution)/shard_map/pallas_call | solution.py:148
  109.8 5.2 %shard_map.43.refs_5_ = f32[3,512,384]{2,1,0:T(8,128)S(1)} custom-call(s32[9]{0:T(128)S(1)} %stack.214.refs_0_, bf16[2,512,384]{2,1,0:T(8,128)(2,1)S(1)} %collective-permute-done.18.refs_1_, bf16[2,512,384]{2,1,0:T(8,128)(2,1)S(1)} %collective-permute-done.19.refs_2_, bf16[3,3072,384]{2,1,0:T(8,128)(2,1)S(1)} %bitcast.51, ...), custom_call_target="tpu_custom_call", output_to_operand_aliasing={{}: (5, {})} | custom-call | flops 1811939328 | bytes 5111808 | tf_op jit(solution)/shard_map/pallas_call | solution.py:148
  115.0 6.1 %shard_map.44 = bf16[512,384]{1,0:T(8,128)(2,1)} custom-call(s32[9]{0:T(128)S(1)} %stack.200.refs_0_, bf16[2,512,384]{2,1,0:T(8,128)(2,1)S(1)} %collective-permute-done.13.refs_1_, bf16[2,512,384]{2,1,0:T(8,128)(2,1)S(1)} %collective-permute-done.17.refs_2_, bf16[3,3072,384]{2,1,0:T(8,128)(2,1)S(1)} %bitcast.52, ...), custom_call_target="tpu_custom_call" | custom-call | flops 1811939328 | bytes 5111808 | tf_op jit(solution)/shard_map/pallas_call | solution.py:148
  (32 shorter events, 1.1 us)
Async XLA Ops:
  0.0 31.4 %collective-permute-start.7 = (bf16[3,3072,384]{2,1,0:T(8,128)(2,1)}, bf16[3,3072,384]{2,1,0:T(8,128)(2,1)}, u32[]{:S(2)}, u32[]{:S(2)}) collective-permute-start(bf16[3,3072,384]{2,1,0:T(8,128)(2,1)} %bitcast.44), channel_id=1, source_target_pairs={{0,16},{16,0},{1,17},{17,1},{2,18},{18,2},{3,19},{19,3},{4,20},{20... | collective-permute-start | bytes 21233672 | tf_op jit(solution)/shard_map/ppermute | solution.py:188
  0.0 12.6 %collective-permute-start.3 = (bf16[512,384]{1,0:T(8,128)(2,1)}, bf16[512,384]{1,0:T(8,128)(2,1)S(1)}, u32[]{:S(2)}, u32[]{:S(2)}) collective-permute-start(bf16[512,384]{1,0:T(8,128)(2,1)} %bitcast.53), channel_id=1, source_target_pairs={{0,3},{1,0},{2,1},{3,2},{4,7},{5,4},{6,5},{7,6},{8,11},{9,8},{10,9... | collective-permute-start | bytes 1179656 | tf_op jit(solution)/shard_map/ppermute | solution.py:29
  2.8 9.9 %collective-permute-start.4 = (bf16[512,384]{1,0:T(8,128)(2,1)}, bf16[512,384]{1,0:T(8,128)(2,1)S(1)}, u32[]{:S(2)}, u32[]{:S(2)}) collective-permute-start(bf16[512,384]{1,0:T(8,128)(2,1)} %bitcast.54), channel_id=1, source_target_pairs={{0,2},{1,3},{2,0},{3,1},{4,6},{5,7},{6,4},{7,5},{8,10},{9,11},{10,... | collective-permute-start | bytes 1179656 | tf_op jit(solution)/shard_map/ppermute | solution.py:29
  3.6 12.9 %collective-permute-start = (bf16[512,384]{1,0:T(8,128)(2,1)}, bf16[512,384]{1,0:T(8,128)(2,1)S(1)}, u32[]{:S(2)}, u32[]{:S(2)}) collective-permute-start(bf16[512,384]{1,0:T(8,128)(2,1)} %bitcast.55), channel_id=1, source_target_pairs={{0,1},{1,2},{2,3},{3,0},{4,5},{5,6},{6,7},{7,4},{8,9},{9,10},{10,1... | collective-permute-start | bytes 1179656 | tf_op jit(solution)/shard_map/ppermute | solution.py:29
  12.7 13.3 %collective-permute-start.5 = (bf16[2,512,384]{2,1,0:T(8,128)(2,1)S(1)}, bf16[2,512,384]{2,1,0:T(8,128)(2,1)S(1)}, u32[]{:S(2)}, u32[]{:S(2)}) collective-permute-start(bf16[2,512,384]{2,1,0:T(8,128)(2,1)S(1)} %pad_maximum_fusion.1.refs_2_), channel_id=1, source_target_pairs={{0,12},{1,13},{2,14},{3,15},{4,0},{5,1},{6,2},{7,3},{8,4},{9,5},{1... | collective-permute-start | bytes 2359304 | tf_op jit(solution)/shard_map/ppermute | solution.py:29
  17.6 12.1 %collective-permute-start.1 = (bf16[2,512,384]{2,1,0:T(8,128)(2,1)S(1)}, bf16[2,512,384]{2,1,0:T(8,128)(2,1)S(1)}, u32[]{:S(2)}, u32[]{:S(2)}) collective-permute-start(bf16[2,512,384]{2,1,0:T(8,128)(2,1)S(1)} %pad_maximum_fusion.refs_1_), channel_id=1, source_target_pairs={{0,4},{1,5},{2,6},{3,7},{4,8},{5,9},{6,10},{7,11},{8,12},{9,13},{1... | collective-permute-start | bytes 2359304 | tf_op jit(solution)/shard_map/ppermute | solution.py:29
  17.9 27.2 %collective-permute-start.8 = (bf16[2,512,384]{2,1,0:T(8,128)(2,1)S(1)}, bf16[2,512,384]{2,1,0:T(8,128)(2,1)}, u32[]{:S(2)}, u32[]{:S(2)}) collective-permute-start(bf16[2,512,384]{2,1,0:T(8,128)(2,1)S(1)} %pad_maximum_fusion.1.refs_2_), channel_id=1, source_target_pairs={{0,4},{1,5},{2,6},{3,7},{4,8},{5,9},{6,10},{7,11},{8,12},{9,13},{1... | collective-permute-start | bytes 2359304 | tf_op jit(solution)/shard_map/ppermute | solution.py:29
  19.4 25.7 %collective-permute-start.9 = (bf16[2,512,384]{2,1,0:T(8,128)(2,1)S(1)}, bf16[2,512,384]{2,1,0:T(8,128)(2,1)}, u32[]{:S(2)}, u32[]{:S(2)}) collective-permute-start(bf16[2,512,384]{2,1,0:T(8,128)(2,1)S(1)} %pad_maximum_fusion.refs_1_), channel_id=1, source_target_pairs={{0,12},{1,13},{2,14},{3,15},{4,0},{5,1},{6,2},{7,3},{8,4},{9,5},{1... | collective-permute-start | bytes 2359304 | tf_op jit(solution)/shard_map/ppermute | solution.py:29
  26.0 24.4 %collective-permute-start.6 = (bf16[2,512,384]{2,1,0:T(8,128)(2,1)S(1)}, bf16[2,512,384]{2,1,0:T(8,128)(2,1)}, u32[]{:S(2)}, u32[]{:S(2)}) collective-permute-start(bf16[2,512,384]{2,1,0:T(8,128)(2,1)S(1)} %collective-permute-done.5.refs_2_), channel_id=1, source_target_pairs={{0,12},{1,13},{2,14},{3,15},{4,0},{5,1},{6,2},{7,3},{8,4},{9,5},{1... | collective-permute-start | bytes 2359304 | tf_op jit(solution)/shard_map/ppermute | solution.py:29
  29.6 20.7 %collective-permute-start.2 = (bf16[2,512,384]{2,1,0:T(8,128)(2,1)S(1)}, bf16[2,512,384]{2,1,0:T(8,128)(2,1)}, u32[]{:S(2)}, u32[]{:S(2)}) collective-permute-start(bf16[2,512,384]{2,1,0:T(8,128)(2,1)S(1)} %collective-permute-done.1.refs_1_), channel_id=1, source_target_pairs={{0,4},{1,5},{2,6},{3,7},{4,8},{5,9},{6,10},{7,11},{8,12},{9,13},{1... | collective-permute-start | bytes 2359304 | tf_op jit(solution)/shard_map/ppermute | solution.py:29
  31.4 3.0 %copy-start = (bf16[1,3,3072,384]{3,2,1,0:T(8,128)(2,1)S(1)}, bf16[1,3,3072,384]{3,2,1,0:T(8,128)(2,1)}, u32[]{:S(2)}) copy-start(bf16[1,3,3072,384]{3,2,1,0:T(8,128)(2,1)} %param.5) | copy-start | bytes 21233668
  34.4 5.4 %copy-start.1 = (bf16[1,3,3072,384]{3,2,1,0:T(8,128)(2,1)S(1)}, bf16[1,3,3072,384]{3,2,1,0:T(8,128)(2,1)}, u32[]{:S(2)}) copy-start(bf16[1,3,3072,384]{3,2,1,0:T(8,128)(2,1)} %param.5) | copy-start | bytes 21233668
  45.1 5.3 %copy-start.2 = (bf16[1,512,384]{2,1,0:T(8,128)(2,1)S(1)}, bf16[1,512,384]{2,1,0:T(8,128)(2,1)}, u32[]{:S(2)}) copy-start(bf16[1,512,384]{2,1,0:T(8,128)(2,1)} %param.3) | copy-start | bytes 1179652
  45.1 5.3 %copy-start.3 = (bf16[1,512,384]{2,1,0:T(8,128)(2,1)S(1)}, bf16[1,512,384]{2,1,0:T(8,128)(2,1)}, u32[]{:S(2)}) copy-start(bf16[1,512,384]{2,1,0:T(8,128)(2,1)} %param.4) | copy-start | bytes 1179652
  55.5 12.6 %collective-permute-start.10 = (bf16[512,384]{1,0:T(8,128)(2,1)S(1)}, bf16[512,384]{1,0:T(8,128)(2,1)S(1)}, u32[]{:S(2)}, u32[]{:S(2)}) collective-permute-start(bf16[512,384]{1,0:T(8,128)(2,1)S(1)} %shard_map.40), channel_id=1, source_target_pairs={{0,32},{32,64},{64,96},{96,128},{128,160},{160,192},{192,224},{224... | collective-permute-start | bytes 1179656 | tf_op jit(solution)/shard_map/ppermute | solution.py:193
  68.0 12.5 %collective-permute-start.14 = (bf16[512,384]{1,0:T(8,128)(2,1)S(1)}, bf16[512,384]{1,0:T(8,128)(2,1)S(1)}, u32[]{:S(2)}, u32[]{:S(2)}) collective-permute-start(bf16[512,384]{1,0:T(8,128)(2,1)S(1)} %collective-permute-done.10.refs_6_), channel_id=1, source_target_pairs={{0,3},{1,0},{2,1},{3,2},{4,7},{5,4},{6,5},{7,6},{8,11},{9,8},{10,9... | collective-permute-start | bytes 1179656 | tf_op jit(solution)/shard_map/ppermute | solution.py:29
  71.0 9.5 %collective-permute-start.15 = (bf16[512,384]{1,0:T(8,128)(2,1)S(1)}, bf16[512,384]{1,0:T(8,128)(2,1)S(1)}, u32[]{:S(2)}, u32[]{:S(2)}) collective-permute-start(bf16[512,384]{1,0:T(8,128)(2,1)S(1)} %collective-permute-done.10.refs_6_), channel_id=1, source_target_pairs={{0,2},{1,3},{2,0},{3,1},{4,6},{5,7},{6,4},{7,5},{8,10},{9,11},{10,... | collective-permute-start | bytes 1179656 | tf_op jit(solution)/shard_map/ppermute | solution.py:29
  71.0 13.2 %collective-permute-start.11 = (bf16[512,384]{1,0:T(8,128)(2,1)S(1)}, bf16[512,384]{1,0:T(8,128)(2,1)S(1)}, u32[]{:S(2)}, u32[]{:S(2)}) collective-permute-start(bf16[512,384]{1,0:T(8,128)(2,1)S(1)} %collective-permute-done.10.refs_6_), channel_id=1, source_target_pairs={{0,1},{1,2},{2,3},{3,0},{4,5},{5,6},{6,7},{7,4},{8,9},{9,10},{10,1... | collective-permute-start | bytes 1179656 | tf_op jit(solution)/shard_map/ppermute | solution.py:29
  80.6 13.3 %collective-permute-start.16 = (bf16[2,512,384]{2,1,0:T(8,128)(2,1)S(1)}, bf16[2,512,384]{2,1,0:T(8,128)(2,1)S(1)}, u32[]{:S(2)}, u32[]{:S(2)}) collective-permute-start(bf16[2,512,384]{2,1,0:T(8,128)(2,1)S(1)} %pad_maximum_fusion.3.refs_2_), channel_id=1, source_target_pairs={{0,12},{1,13},{2,14},{3,15},{4,0},{5,1},{6,2},{7,3},{8,4},{9,5},{1... | collective-permute-start | bytes 2359304 | tf_op jit(solution)/shard_map/ppermute | solution.py:29
  84.3 12.1 %collective-permute-start.12 = (bf16[2,512,384]{2,1,0:T(8,128)(2,1)S(1)}, bf16[2,512,384]{2,1,0:T(8,128)(2,1)S(1)}, u32[]{:S(2)}, u32[]{:S(2)}) collective-permute-start(bf16[2,512,384]{2,1,0:T(8,128)(2,1)S(1)} %pad_maximum_fusion.2.refs_1_), channel_id=1, source_target_pairs={{0,4},{1,5},{2,6},{3,7},{4,8},{5,9},{6,10},{7,11},{8,12},{9,13},{1... | collective-permute-start | bytes 2359304 | tf_op jit(solution)/shard_map/ppermute | solution.py:29
  86.1 23.6 %collective-permute-start.18 = (bf16[2,512,384]{2,1,0:T(8,128)(2,1)S(1)}, bf16[2,512,384]{2,1,0:T(8,128)(2,1)S(1)}, u32[]{:S(2)}, u32[]{:S(2)}) collective-permute-start(bf16[2,512,384]{2,1,0:T(8,128)(2,1)S(1)} %pad_maximum_fusion.3.refs_2_), channel_id=1, source_target_pairs={{0,4},{1,5},{2,6},{3,7},{4,8},{5,9},{6,10},{7,11},{8,12},{9,13},{1... | collective-permute-start | bytes 2359304 | tf_op jit(solution)/shard_map/ppermute | solution.py:29
  86.2 23.5 %collective-permute-start.19 = (bf16[2,512,384]{2,1,0:T(8,128)(2,1)S(1)}, bf16[2,512,384]{2,1,0:T(8,128)(2,1)S(1)}, u32[]{:S(2)}, u32[]{:S(2)}) collective-permute-start(bf16[2,512,384]{2,1,0:T(8,128)(2,1)S(1)} %pad_maximum_fusion.2.refs_1_), channel_id=1, source_target_pairs={{0,12},{1,13},{2,14},{3,15},{4,0},{5,1},{6,2},{7,3},{8,4},{9,5},{1... | collective-permute-start | bytes 2359304 | tf_op jit(solution)/shard_map/ppermute | solution.py:29
  93.9 21.1 %collective-permute-start.17 = (bf16[2,512,384]{2,1,0:T(8,128)(2,1)S(1)}, bf16[2,512,384]{2,1,0:T(8,128)(2,1)S(1)}, u32[]{:S(2)}, u32[]{:S(2)}) collective-permute-start(bf16[2,512,384]{2,1,0:T(8,128)(2,1)S(1)} %collective-permute-done.16.refs_2_), channel_id=1, source_target_pairs={{0,12},{1,13},{2,14},{3,15},{4,0},{5,1},{6,2},{7,3},{8,4},{9,5},{1... | collective-permute-start | bytes 2359304 | tf_op jit(solution)/shard_map/ppermute | solution.py:29
  96.3 18.7 %collective-permute-start.13 = (bf16[2,512,384]{2,1,0:T(8,128)(2,1)S(1)}, bf16[2,512,384]{2,1,0:T(8,128)(2,1)S(1)}, u32[]{:S(2)}, u32[]{:S(2)}) collective-permute-start(bf16[2,512,384]{2,1,0:T(8,128)(2,1)S(1)} %collective-permute-done.12.refs_1_), channel_id=1, source_target_pairs={{0,4},{1,5},{2,6},{3,7},{4,8},{5,9},{6,10},{7,11},{8,12},{9,13},{1... | collective-permute-start | bytes 2359304 | tf_op jit(solution)/shard_map/ppermute | solution.py:29

commit v2 on v0

v2 whole, which is shorter than its diff:
```python
import functools

import jax
import jax.numpy as jnp
from jax import lax
from jax.experimental import pallas as pl
from jax.experimental.pallas import tpu as pltpu
from jax.sharding import PartitionSpec as P

SIDE = 4
PLANE = ("row", "col")
NEAR = (0, -1, 1, 2)
VMEM = pl.BlockSpec(memory_space=pltpu.VMEM)
ANY = pl.BlockSpec(memory_space=pl.ANY)


def ring_pairs(step, first):
    pairs = []
    for core in range(2):
        for col in range(SIDE * SIDE):
            y, x = divmod(col, SIDE)
            if (core == 0) == first:
                x = (x + step) % SIDE
            else:
                y = (y + step) % SIDE
            pairs.append((core * SIDE * SIDE + col, core * SIDE * SIDE + y * SIDE + x))
    return pairs


def shift(value, step, first):
    return lax.ppermute(value, PLANE, ring_pairs(step, first))


def relay(output):
    count = lax.axis_size("section")
    return lax.ppermute(output, "section", [(s, (s + 1) % count) for s in range(count)])


def block_ids():
    core, col = lax.axis_index("row"), lax.axis_index("col")
    y, x = col // SIDE, col % SIDE
    ids = []
    for second in NEAR:
        for first in NEAR:
            along_x = first + core * (second - first)
            along_y = second + core * (first - second)
            block = (y + along_y + SIDE) % SIDE * SIDE + (x + along_x + SIDE) % SIDE
            ids.append(((block // 8 + core) % 2, block % 8))
    return ids


def in_vmem(value):
    return pltpu.with_memory_space_constraint(value, pltpu.VMEM)


def in_hbm(value):
    return pltpu.with_memory_space_constraint(value, pltpu.HBM)


def run(kernel, out_shape, operands, after=(), specs=None, scratch=(), megabytes=4):
    operands = list(operands)
    if specs is None:
        specs = [VMEM] * len(operands)
        operands = [in_vmem(v) for v in operands]
    count = len(operands)

    def body(*refs):
        kernel(*refs[:count], *refs[count + len(after) :])

    return pl.pallas_call(
        body,
        out_shape=out_shape,
        in_specs=specs + [VMEM] * len(after),
        out_specs=jax.tree.map(lambda _: VMEM, out_shape),
        scratch_shapes=list(scratch),
        compiler_params=pltpu.CompilerParams(vmem_limit_bytes=megabytes * 1024 * 1024),
        cost_estimate=pl.CostEstimate(flops=1, bytes_accessed=1, transcendentals=0),
    )(*operands, *map(in_vmem, after))


def arrange(own, other, after):
    _, half, width = own.shape
    depth = half // 8

    def kernel(own, other, out, sems):
        ids = block_ids()

        def copy(source, block, k):
            rows = pl.ds(pl.multiple_of(ids[block][1] * depth, depth), depth)
            place = out.at[pl.ds(block * depth, depth), pl.ds(k * width, width)]
            return pltpu.make_async_copy(source.at[k, rows, :], place, sems.at[block, k])

        for block in range(SIDE * SIDE):

            @pl.when(ids[block][0] == 0)
            def _():
                for k in range(3):
                    copy(own, block, k).start()

            @pl.when(ids[block][0] != 0)
            def _():
                for k in range(3):
                    copy(other, block, k).start()

        for block in range(SIDE * SIDE):
            for k in range(3):
                copy(own, block, k).wait()

    return run(
        kernel,
        pltpu.VMEM((2 * half, 3 * width), jnp.bfloat16),
        [in_hbm(own), in_vmem(other)],
        after,
        specs=[ANY, VMEM],
        scratch=[pltpu.SemaphoreType.DMA((SIDE * SIDE, 3))],
    )


def bring_in(values):
    def kernel(*refs):
        sems = refs[-1]
        count = len(values)
        copies = [
            pltpu.make_async_copy(refs[i], refs[count + i], sems.at[i]) for i in range(count)
        ]
        for copy in copies:
            copy.start()
        for copy in copies:
            copy.wait()

    return run(
        kernel,
        tuple(pltpu.VMEM(v.shape, v.dtype) for v in values),
        [in_hbm(v) for v in values],
        specs=[ANY] * len(values),
        scratch=[pltpu.SemaphoreType.DMA((len(values),))],
    )


def stack(parts, cut, after):
    def kernel(*refs):
        for i, ref in enumerate(refs[:-1]):
            refs[-1][i] = ref[cut]

    tokens, width = cut.stop - cut.start, parts[0].shape[1]
    return run(kernel, pltpu.VMEM((len(parts), tokens, width), jnp.bfloat16), parts, after)


def pick(up, down, after):
    def kernel(up, down, far_up, far_down):
        far_up[...] = up[:2]
        far_down[...] = down[2:]

    one = pltpu.VMEM((2, *up.shape[1:]), jnp.bfloat16)
    return run(kernel, (one, one), [up, down], after)


def same(value, after):
    def kernel(value, out):
        out[...] = value[...]

    return run(kernel, pltpu.VMEM(value.shape, value.dtype), [value], after)


def gathered(refs):
    return jnp.concatenate([ref[i] for ref in refs for i in range(ref.shape[0])], axis=1)


def nearest(near, weights, after):
    def kernel(near, weights, out):
        acts = gathered((near,))
        out[...] = jnp.dot(acts, weights[: acts.shape[1]], preferred_element_type=jnp.float32)

    tokens, width = near.shape[1:]
    kind = pltpu.VMEM((tokens, 3 * width), jnp.float32)
    return run(kernel, kind, [near, weights], after, megabytes=16)


def next_ones(up, down, weights, acc, after):
    def kernel(up, down, weights, acc, out):
        acts = gathered((up, down))
        rows = slice(acts.shape[1] // 2, acts.shape[1] * 3 // 2)
        out[...] = acc[...] + jnp.dot(acts, weights[rows], preferred_element_type=jnp.float32)

    kind = pltpu.VMEM(acc.shape, acc.dtype)
    return run(kernel, kind, [up, down, weights, acc], after, megabytes=16)


def finished(far_up, far_down, weights, acc, acts):
    far = gathered((far_up, far_down))
    width = acts.shape[1]
    start = weights.shape[0] - far.shape[1]
    total = acc[...] + jnp.dot(far, weights[start:], preferred_element_type=jnp.float32)
    first, second, third = (total[:, k * width : (k + 1) * width] for k in range(3))
    gate = 1.0 / (1.0 + jnp.exp(-third))
    cubic = 0.7978845608 * (first + 0.044715 * (first * first * first))
    value = acts.astype(jnp.float32) + gate * (0.5 * first * (1.0 + jnp.tanh(cubic))) * second
    return value.astype(jnp.bfloat16)


def hand_on(parts, weights, acc, acts, injected, cut, after):
    def kernel(far_up, far_down, weights, acc, acts, injected, out):
        value = finished(far_up, far_down, weights, acc, acts[cut])
        last = lax.axis_index("section") == lax.axis_size("section") - 1
        out[...] = jnp.where(last, injected[cut], value)

    return run(
        kernel,
        pltpu.VMEM(parts[0].shape[1:], jnp.bfloat16),
        [*parts, weights, acc, acts, injected],
        after,
        megabytes=16,
    )


def conclude(parts, weights, acc, acts, before, after):
    def kernel(far_up, far_down, weights, acc, acts, *refs):
        out = refs[-1]
        done = 0
        for ref in refs[:-1]:
            out[done : done + ref.shape[0]] = ref[...]
            done += ref.shape[0]
        out[done:] = finished(far_up, far_down, weights, acc, acts[...])

    tokens, width = acts.shape
    tokens += sum(v.shape[0] for v in before)
    kind = pltpu.VMEM if not before else jax.ShapeDtypeStruct
    return run(
        kernel,
        kind((tokens, width), jnp.bfloat16),
        [*parts, weights, acc, acts, *before],
        after,
        megabytes=16,
    )


def second_phase(near):
    return shift(near, 1, False), shift(near, 3, False)


def third_phase(up, down, after):
    far_up, far_down = pick(up, down, after)
    return (shift(far_up, 1, False), shift(far_down, 3, False)), far_up


def body(in_flight, injected, weights):
    own = weights[0]
    other = lax.ppermute(own, "row", [(0, 1), (1, 0)])
    acts, injected = in_flight[0], injected[0]
    half = acts.shape[0] // 2
    low, high = slice(0, half), slice(half, 2 * half)
    whole = slice(0, half)

    blocks = [shift(acts, step, True) for step in (1, 3)]
    acts, injected = bring_in([acts, injected])
    blocks = [acts, *blocks, shift(acts, 2, True)]
    near_a = stack(blocks, low, [])
    moved_a = second_phase(near_a)
    arranged = arrange(own, other, [near_a])
    near_b = stack(blocks, high, [arranged])
    moved_b = second_phase(near_b)
    acc_a = nearest(near_a, arranged, [near_b])
    acc_b = nearest(near_b, arranged, [acc_a])
    far_a, sent = third_phase(*moved_a, [acc_b])
    acc_a = next_ones(*moved_a, arranged, acc_a, [sent])
    far_b, sent = third_phase(*moved_b, [acc_a])
    out_a = hand_on(far_a, arranged, acc_a, acts, injected, low, [sent])
    acc_b = next_ones(*moved_b, arranged, acc_b, [out_a])
    out_b = hand_on(far_b, arranged, acc_b, acts, injected, high, [])

    acts_a = same(relay(out_a), [out_b])
    acts_b = same(relay(out_b), [acts_a])
    blocks = [acts_a] + [shift(acts_a, step, True) for step in (1, 3, 2)]
    near_a = stack(blocks, whole, [acts_b])
    moved_a = second_phase(near_a)
    blocks = [acts_b] + [shift(acts_b, step, True) for step in (1, 3, 2)]
    near_b = stack(blocks, whole, [near_a])
    moved_b = second_phase(near_b)
    acc_a = nearest(near_a, arranged, [near_b])
    acc_b = nearest(near_b, arranged, [acc_a])
    far_a, sent = third_phase(*moved_a, [acc_b])
    acc_a = next_ones(*moved_a, arranged, acc_a, [sent])
    far_b, sent = third_phase(*moved_b, [acc_a])
    out_a = conclude(far_a, arranged, acc_a, acts_a, [], [sent])
    acc_b = next_ones(*moved_b, arranged, acc_b, [out_a])
    return conclude(far_b, arranged, acc_b, acts_b, [out_a], [])[None]


def solution(mesh):
    placed = (P("section", "row", "col"), P(None, "row", "col"), P("section", None, "row", "col"))
    return jax.shard_map(
        body, mesh=mesh, in_specs=placed, out_specs=P("section", "row", "col"), check_vma=False
    )
```

time: 235 us -> 96.3 us (0.41)
  waiting for transfers between devices: 179 us -> 37 us
  starting transfers between devices: 3.56 us -> 33.9 us
  Pallas kernels: 0 us -> 25.1 us
  matrix products: 24.2 us -> 0 us
  between operations: 13.2 us -> 0.19 us
  local copies, waits for them, and re-layouts: 12.5 us -> 0 us
    all_gather x3 -> x0, waiting for transfers between devices: 169 us -> none  [the longest x2 136 us: panel_products(): lax.all_gather(acts, 'col', axis=1, tiled=True)]
    ppermute x1 -> x28, starting transfers between devices: 3.48 us -> 33.9 us  [the longest x25 32.8 us: shift(): return lax.ppermute(value, PLANE, ring_pairs(step, first))]
    ppermute x1 -> x28, waiting for transfers between devices: 8.58 us -> 37 us  [the longest x25 34.3 us: shift(): return lax.ppermute(value, PLANE, ring_pairs(step, first))]
    pallas_call x0 -> x24, Pallas kernels: none -> 25.1 us  [run(): pl.pallas_call(body, out_shape=out_shape, in_specs=specs + [VMEM] * len(a...]
    dot_general x2 -> x0, matrix products: 24.2 us -> none  [panel_products(): jnp.einsum('tf,kfo->kto', lax.all_gather(acts, 'col', axis=1, tiled=True)...]
    unnamed x9 -> x0, local copies, waits for them, and re-layouts: 11.6 us -> none
  transfers between devices with their start and end apart: 4 -> 28, of which waited for: 4 -> 22; matrix products, arithmetic and copies ran while one was open for 5% -> 0% of each run, Pallas kernels for 0% -> 24%
where the time goes in v2:
time: 96.3 us; the launch traced here: 96.2 us
  waiting for transfers between devices  37 us (38%)
  starting transfers between devices  33.9 us (35%)
  Pallas kernels  25.1 us (26%)
    ppermute x25, waiting for transfers between devices, shift(): return lax.ppermute(value, PLANE, ring_pairs(step, first))  34.3 us
    ppermute x25, starting transfers between devices, shift(): return lax.ppermute(value, PLANE, ring_pairs(step, first))  32.8 us
    pallas_call x24, Pallas kernels, run(): pl.pallas_call(body, out_shape=out_shape, in_specs=specs + [VMEM] * len(a...  25.1 us
    ppermute x2, waiting for transfers between devices, relay(): lax.ppermute(output, 'section', [(s, (s + 1) % count) for s in range(coun...  2.7 us
  transfers between devices with their start and end apart: 28, of which 22 were waited for; matrix products, arithmetic and copies ran while one was open for 0% of the time, Pallas kernels for 24%

profile of v2, /device:TPU:24, one launch (start us, length us, event | category | flops | bytes accessed | tf_op | source)
XLA Modules:
  0.0 96.2 jit_solution(2449719570142085072)
XLA Ops:
  1.1 3.1 %collective-permute-start.2 = (bf16[512,384]{1,0:T(8,128)(2,1)S(1)}, bf16[512,384]{1,0:T(8,128)(2,1)S(1)}, u32[]{:S(2)}, u32[]{:S(2)}) collective-permute-start(bf16[512,384]{1,0:T(8,128)(2,1)S(1)} %get-tuple-element.15.refs_0_.refs_4_), channel_id=1, source_target_pairs={{0,2},{1,3},{2,0},{3,1},{4,6},{5,7},{6,4},{7,5},{8,10},{9,11},{10,... | collective-permute-start | bytes 1179656 | tf_op jit(solution)/shard_map/ppermute | solution.py:31
  4.8 2.6 %collective-permute-start.1 = (bf16[512,384]{1,0:T(8,128)(2,1)}, bf16[512,384]{1,0:T(8,128)(2,1)S(1)}, u32[]{:S(2)}, u32[]{:S(2)}) collective-permute-start(bf16[512,384]{1,0:T(8,128)(2,1)} %bitcast.9), channel_id=1, source_target_pairs={{0,3},{1,0},{2,1},{3,2},{4,7},{5,4},{6,5},{7,6},{8,11},{9,8},{10,9... | collective-permute-start | bytes 1179656 | tf_op jit(solution)/shard_map/ppermute | solution.py:31
  7.5 3.1 %collective-permute-done.2.refs_3_ = bf16[512,384]{1,0:T(8,128)(2,1)S(1)} collective-permute-done((bf16[512,384]{1,0:T(8,128)(2,1)S(1)}, bf16[512,384]{1,0:T(8,128)(2,1)S(1)}, u32[]{:S(2)}, u32[]{:S(2)}) %collective-permute-start.2) | collective-permute-done | bytes 393248 | tf_op jit(solution)/shard_map/ppermute | solution.py:31
  10.6 4.1 %collective-permute-done.refs_1_ = bf16[512,384]{1,0:T(8,128)(2,1)S(1)} collective-permute-done((bf16[512,384]{1,0:T(8,128)(2,1)}, bf16[512,384]{1,0:T(8,128)(2,1)S(1)}, u32[]{:S(2)}, u32[]{:S(2)}) %collective-permute-start) | collective-permute-done | bytes 393248 | tf_op jit(solution)/shard_map/ppermute | solution.py:31
  14.9 2.0 %collective-permute-start.6 = (bf16[4,256,384]{2,1,0:T(8,128)(2,1)S(1)}, bf16[4,256,384]{2,1,0:T(8,128)(2,1)S(1)}, u32[]{:S(2)}, u32[]{:S(2)}) collective-permute-start(bf16[4,256,384]{2,1,0:T(8,128)(2,1)S(1)} %shard_map.38.refs_2_.refs_0_), channel_id=1, source_target_pairs={{0,4},{1,5},{2,6},{3,7},{4,8},{5,9},{6,10},{7,11},{8,12},{9,13},{1... | collective-permute-start | bytes 2359304 | tf_op jit(solution)/shard_map/ppermute | solution.py:31
  17.0 4.3 %shard_map.39.refs_4_.refs_1_.refs_2_ = bf16[6144,1152]{1,0:T(8,128)(2,1)S(1)} custom-call(bf16[3,3072,384]{2,1,0:T(8,128)(2,1)} %bitcast.5, bf16[3,3072,384]{2,1,0:T(8,128)(2,1)S(1)} %collective-permute-done.3.refs_1_, bf16[4,256,384]{2,1,0:T(8,128)(2,1)S(1)} %shard_map.38.refs_2_.refs_0_), custom_call_target="tpu_custom_call" | custom-call | flops 1 | bytes 1 | tf_op jit(solution)/shard_map/pallas_call | solution.py:70
  21.4 2.4 %collective-permute-start.4 = (bf16[4,256,384]{2,1,0:T(8,128)(2,1)S(1)}, bf16[4,256,384]{2,1,0:T(8,128)(2,1)S(1)}, u32[]{:S(2)}, u32[]{:S(2)}) collective-permute-start(bf16[4,256,384]{2,1,0:T(8,128)(2,1)S(1)} %shard_map.40.refs_2_.refs_0_), channel_id=1, source_target_pairs={{0,4},{1,5},{2,6},{3,7},{4,8},{5,9},{6,10},{7,11},{8,12},{9,13},{1... | collective-permute-start | bytes 2359304 | tf_op jit(solution)/shard_map/ppermute | solution.py:31
  26.9 3.1 %collective-permute-done.7.refs_1_ = bf16[4,256,384]{2,1,0:T(8,128)(2,1)S(1)} collective-permute-done((bf16[4,256,384]{2,1,0:T(8,128)(2,1)S(1)}, bf16[4,256,384]{2,1,0:T(8,128)(2,1)S(1)}, u32[]{:S(2)}, u32[]{:S(2)}) %collective-permute-start.7) | collective-permute-done | bytes 786464 | tf_op jit(solution)/shard_map/ppermute | solution.py:31
  30.2 2.0 %collective-permute-start.11 = (bf16[2,256,384]{2,1,0:T(8,128)(2,1)S(1)}, bf16[2,256,384]{2,1,0:T(8,128)(2,1)S(1)}, u32[]{:S(2)}, u32[]{:S(2)}) collective-permute-start(bf16[2,256,384]{2,1,0:T(8,128)(2,1)S(1)} %get-tuple-element.19), channel_id=1, source_target_pairs={{0,12},{1,13},{2,14},{3,15},{4,0},{5,1},{6,2},{7,3},{8,4},{9,5},{1... | collective-permute-start | bytes 1179656 | tf_op jit(solution)/shard_map/ppermute | solution.py:31
  32.2 2.2 %shard_map.44.refs_2_.refs_3_ = f32[256,1152]{1,0:T(8,128)S(1)} custom-call(bf16[4,256,384]{2,1,0:T(8,128)(2,1)S(1)} %collective-permute-done.6.refs_0_, bf16[4,256,384]{2,1,0:T(8,128)(2,1)S(1)} %collective-permute-done.7.refs_1_, bf16[6144,1152]{1,0:T(8,128)(2,1)S(1)} %shard_map.39.refs_4_.refs_1_.refs_2_, f32[256,1152]{1,0:T(8,128)S(1)} %shard_map.41.refs_2_.refs_3_, ...), custom_call_target="tpu_custom_call" | custom-call | flops 1 | bytes 1 | tf_op jit(solution)/shard_map/pallas_call | solution.py:70
  35.4 3.1 %collective-permute-done.5.refs_1_ = bf16[4,256,384]{2,1,0:T(8,128)(2,1)S(1)} collective-permute-done((bf16[4,256,384]{2,1,0:T(8,128)(2,1)S(1)}, bf16[4,256,384]{2,1,0:T(8,128)(2,1)S(1)}, u32[]{:S(2)}, u32[]{:S(2)}) %collective-permute-start.5) | collective-permute-done | bytes 786464 | tf_op jit(solution)/shard_map/ppermute | solution.py:31
  38.6 2.0 %collective-permute-start.9 = (bf16[2,256,384]{2,1,0:T(8,128)(2,1)S(1)}, bf16[2,256,384]{2,1,0:T(8,128)(2,1)S(1)}, u32[]{:S(2)}, u32[]{:S(2)}) collective-permute-start(bf16[2,256,384]{2,1,0:T(8,128)(2,1)S(1)} %get-tuple-element.18), channel_id=1, source_target_pairs={{0,12},{1,13},{2,14},{3,15},{4,0},{5,1},{6,2},{7,3},{8,4},{9,5},{1... | collective-permute-start | bytes 1179656 | tf_op jit(solution)/shard_map/ppermute | solution.py:31
  40.6 2.0 %collective-permute-done.11.refs_1_ = bf16[2,256,384]{2,1,0:T(8,128)(2,1)S(1)} collective-permute-done((bf16[2,256,384]{2,1,0:T(8,128)(2,1)S(1)}, bf16[2,256,384]{2,1,0:T(8,128)(2,1)S(1)}, u32[]{:S(2)}, u32[]{:S(2)}) %collective-permute-start.11) | collective-permute-done | bytes 393248 | tf_op jit(solution)/shard_map/ppermute | solution.py:31
  44.2 2.2 %shard_map.47.refs_3_ = f32[256,1152]{1,0:T(8,128)S(1)} custom-call(bf16[4,256,384]{2,1,0:T(8,128)(2,1)S(1)} %collective-permute-done.4.refs_0_, bf16[4,256,384]{2,1,0:T(8,128)(2,1)S(1)} %collective-permute-done.5.refs_1_, bf16[6144,1152]{1,0:T(8,128)(2,1)S(1)} %shard_map.39.refs_4_.refs_1_.refs_2_, f32[256,1152]{1,0:T(8,128)S(1)} %shard_map.42.refs_2_.refs_3_, ...), custom_call_target="tpu_custom_call" | custom-call | flops 1 | bytes 1 | tf_op jit(solution)/shard_map/pallas_call | solution.py:70
  49.7 2.2 %collective-permute-done.13.refs_0_ = bf16[256,384]{1,0:T(8,128)(2,1)S(1)} collective-permute-done((bf16[256,384]{1,0:T(8,128)(2,1)S(1)}, bf16[256,384]{1,0:T(8,128)(2,1)S(1)}, u32[]{:S(2)}, u32[]{:S(2)}) %collective-permute-start.13) | collective-permute-done | bytes 196640 | tf_op jit(solution)/shard_map/ppermute | solution.py:36
  51.9 1.9 %collective-permute-start.17 = (bf16[256,384]{1,0:T(8,128)(2,1)S(1)}, bf16[256,384]{1,0:T(8,128)(2,1)S(1)}, u32[]{:S(2)}, u32[]{:S(2)}) collective-permute-start(bf16[256,384]{1,0:T(8,128)(2,1)S(1)} %shard_map.49.refs_1_.refs_0_.refs_4_), channel_id=1, source_target_pairs={{0,1},{1,2},{2,3},{3,0},{4,5},{5,6},{6,7},{7,4},{8,9},{9,10},{10,1... | collective-permute-start | bytes 589832 | tf_op jit(solution)/shard_map/ppermute | solution.py:31
  57.1 1.6 %collective-permute-start.14 = (bf16[256,384]{1,0:T(8,128)(2,1)S(1)}, bf16[256,384]{1,0:T(8,128)(2,1)S(1)}, u32[]{:S(2)}, u32[]{:S(2)}) collective-permute-start(bf16[256,384]{1,0:T(8,128)(2,1)S(1)} %shard_map.50.refs_4_.refs_0_), channel_id=1, source_target_pairs={{0,1},{1,2},{2,3},{3,0},{4,5},{5,6},{6,7},{7,4},{8,9},{9,10},{10,1... | collective-permute-start | bytes 589832 | tf_op jit(solution)/shard_map/ppermute | solution.py:31
  58.7 1.8 %collective-permute-start.15 = (bf16[256,384]{1,0:T(8,128)(2,1)S(1)}, bf16[256,384]{1,0:T(8,128)(2,1)S(1)}, u32[]{:S(2)}, u32[]{:S(2)}) collective-permute-start(bf16[256,384]{1,0:T(8,128)(2,1)S(1)} %shard_map.50.refs_4_.refs_0_), channel_id=1, source_target_pairs={{0,3},{1,0},{2,1},{3,2},{4,7},{5,4},{6,5},{7,6},{8,11},{9,8},{10,9... | collective-permute-start | bytes 589832 | tf_op jit(solution)/shard_map/ppermute | solution.py:31
  63.2 1.6 %collective-permute-start.23 = (bf16[4,256,384]{2,1,0:T(8,128)(2,1)S(1)}, bf16[4,256,384]{2,1,0:T(8,128)(2,1)S(1)}, u32[]{:S(2)}, u32[]{:S(2)}) collective-permute-start(bf16[4,256,384]{2,1,0:T(8,128)(2,1)S(1)} %shard_map.51.refs_4_.refs_0_), channel_id=1, source_target_pairs={{0,12},{1,13},{2,14},{3,15},{4,0},{5,1},{6,2},{7,3},{8,4},{9,5},{1... | collective-permute-start | bytes 2359304 | tf_op jit(solution)/shard_map/ppermute | solution.py:31
  64.8 1.6 %collective-permute-done.14.refs_1_ = bf16[256,384]{1,0:T(8,128)(2,1)S(1)} collective-permute-done((bf16[256,384]{1,0:T(8,128)(2,1)S(1)}, bf16[256,384]{1,0:T(8,128)(2,1)S(1)}, u32[]{:S(2)}, u32[]{:S(2)}) %collective-permute-start.14) | collective-permute-done | bytes 196640 | tf_op jit(solution)/shard_map/ppermute | solution.py:31
  66.5 3.8 %collective-permute-done.16.refs_3_ = bf16[256,384]{1,0:T(8,128)(2,1)S(1)} collective-permute-done((bf16[256,384]{1,0:T(8,128)(2,1)S(1)}, bf16[256,384]{1,0:T(8,128)(2,1)S(1)}, u32[]{:S(2)}, u32[]{:S(2)}) %collective-permute-start.16) | collective-permute-done | bytes 196640 | tf_op jit(solution)/shard_map/ppermute | solution.py:31
  70.4 2.0 %collective-permute-start.21 = (bf16[4,256,384]{2,1,0:T(8,128)(2,1)S(1)}, bf16[4,256,384]{2,1,0:T(8,128)(2,1)S(1)}, u32[]{:S(2)}, u32[]{:S(2)}) collective-permute-start(bf16[4,256,384]{2,1,0:T(8,128)(2,1)S(1)} %shard_map.52.refs_2_.refs_0_), channel_id=1, source_target_pairs={{0,12},{1,13},{2,14},{3,15},{4,0},{5,1},{6,2},{7,3},{8,4},{9,5},{1... | collective-permute-start | bytes 2359304 | tf_op jit(solution)/shard_map/ppermute | solution.py:31
  74.8 1.6 %collective-permute-done.23.refs_1_ = bf16[4,256,384]{2,1,0:T(8,128)(2,1)S(1)} collective-permute-done((bf16[4,256,384]{2,1,0:T(8,128)(2,1)S(1)}, bf16[4,256,384]{2,1,0:T(8,128)(2,1)S(1)}, u32[]{:S(2)}, u32[]{:S(2)}) %collective-permute-start.23) | collective-permute-done | bytes 786464 | tf_op jit(solution)/shard_map/ppermute | solution.py:31
  76.9 1.7 %collective-permute-start.27 = (bf16[2,256,384]{2,1,0:T(8,128)(2,1)S(1)}, bf16[2,256,384]{2,1,0:T(8,128)(2,1)S(1)}, u32[]{:S(2)}, u32[]{:S(2)}) collective-permute-start(bf16[2,256,384]{2,1,0:T(8,128)(2,1)S(1)} %get-tuple-element.24), channel_id=1, source_target_pairs={{0,12},{1,13},{2,14},{3,15},{4,0},{5,1},{6,2},{7,3},{8,4},{9,5},{1... | collective-permute-start | bytes 1179656 | tf_op jit(solution)/shard_map/ppermute | solution.py:31
  78.6 2.2 %shard_map.56.refs_2_.refs_3_ = f32[256,1152]{1,0:T(8,128)S(1)} custom-call(bf16[4,256,384]{2,1,0:T(8,128)(2,1)S(1)} %collective-permute-done.22.refs_0_, bf16[4,256,384]{2,1,0:T(8,128)(2,1)S(1)} %collective-permute-done.23.refs_1_, bf16[6144,1152]{1,0:T(8,128)(2,1)S(1)} %shard_map.39.refs_4_.refs_1_.refs_2_, f32[256,1152]{1,0:T(8,128)S(1)} %shard_map.53.refs_2_.refs_3_, ...), custom_call_target="tpu_custom_call" | custom-call | flops 1 | bytes 1 | tf_op jit(solution)/shard_map/pallas_call | solution.py:70
  80.8 2.4 %collective-permute-done.20.refs_0_ = bf16[4,256,384]{2,1,0:T(8,128)(2,1)S(1)} collective-permute-done((bf16[4,256,384]{2,1,0:T(8,128)(2,1)S(1)}, bf16[4,256,384]{2,1,0:T(8,128)(2,1)S(1)}, u32[]{:S(2)}, u32[]{:S(2)}) %collective-permute-start.20) | collective-permute-done | bytes 786464 | tf_op jit(solution)/shard_map/ppermute | solution.py:31
  83.2 1.7 %collective-permute-done.21.refs_1_ = bf16[4,256,384]{2,1,0:T(8,128)(2,1)S(1)} collective-permute-done((bf16[4,256,384]{2,1,0:T(8,128)(2,1)S(1)}, bf16[4,256,384]{2,1,0:T(8,128)(2,1)S(1)}, u32[]{:S(2)}, u32[]{:S(2)}) %collective-permute-start.21) | collective-permute-done | bytes 786464 | tf_op jit(solution)/shard_map/ppermute | solution.py:31
  85.3 1.7 %collective-permute-start.25 = (bf16[2,256,384]{2,1,0:T(8,128)(2,1)S(1)}, bf16[2,256,384]{2,1,0:T(8,128)(2,1)S(1)}, u32[]{:S(2)}, u32[]{:S(2)}) collective-permute-start(bf16[2,256,384]{2,1,0:T(8,128)(2,1)S(1)} %get-tuple-element.23), channel_id=1, source_target_pairs={{0,12},{1,13},{2,14},{3,15},{4,0},{5,1},{6,2},{7,3},{8,4},{9,5},{1... | collective-permute-start | bytes 1179656 | tf_op jit(solution)/shard_map/ppermute | solution.py:31
  87.4 1.7 %collective-permute-done.27.refs_1_ = bf16[2,256,384]{2,1,0:T(8,128)(2,1)S(1)} collective-permute-done((bf16[2,256,384]{2,1,0:T(8,128)(2,1)S(1)}, bf16[2,256,384]{2,1,0:T(8,128)(2,1)S(1)}, u32[]{:S(2)}, u32[]{:S(2)}) %collective-permute-start.27) | collective-permute-done | bytes 393248 | tf_op jit(solution)/shard_map/ppermute | solution.py:31
  90.3 2.2 %shard_map.59.refs_3_ = f32[256,1152]{1,0:T(8,128)S(1)} custom-call(bf16[4,256,384]{2,1,0:T(8,128)(2,1)S(1)} %collective-permute-done.20.refs_0_, bf16[4,256,384]{2,1,0:T(8,128)(2,1)S(1)} %collective-permute-done.21.refs_1_, bf16[6144,1152]{1,0:T(8,128)(2,1)S(1)} %shard_map.39.refs_4_.refs_1_.refs_2_, f32[256,1152]{1,0:T(8,128)S(1)} %shard_map.54.refs_2_.refs_3_, ...), custom_call_target="tpu_custom_call" | custom-call | flops 1 | bytes 1 | tf_op jit(solution)/shard_map/pallas_call | solution.py:70
  92.8 1.5 %collective-permute-done.25.refs_1_ = bf16[2,256,384]{2,1,0:T(8,128)(2,1)S(1)} collective-permute-done((bf16[2,256,384]{2,1,0:T(8,128)(2,1)S(1)}, bf16[2,256,384]{2,1,0:T(8,128)(2,1)S(1)}, u32[]{:S(2)}, u32[]{:S(2)}) %collective-permute-start.25) | collective-permute-done | bytes 393248 | tf_op jit(solution)/shard_map/ppermute | solution.py:31
  94.3 2.0 %shard_map.60 = bf16[512,384]{1,0:T(8,128)(2,1)} custom-call(bf16[2,256,384]{2,1,0:T(8,128)(2,1)S(1)} %collective-permute-done.24.refs_0_, bf16[2,256,384]{2,1,0:T(8,128)(2,1)S(1)} %collective-permute-done.25.refs_1_, bf16[6144,1152]{1,0:T(8,128)(2,1)S(1)} %shard_map.39.refs_4_.refs_1_.refs_2_, f32[256,1152]{1,0:T(8,128)S(1)} %shard_map.59.refs_3_, ...), custom_call_target="tpu_custom_call" | custom-call | flops 1 | bytes 1 | tf_op jit(solution)/shard_map/pallas_call | solution.py:70
  (48 shorter events, 22.9 us)
Async XLA Ops:
  0.0 17.0 %collective-permute-start.3 = (bf16[3,3072,384]{2,1,0:T(8,128)(2,1)}, bf16[3,3072,384]{2,1,0:T(8,128)(2,1)S(1)}, u32[]{:S(2)}, u32[]{:S(2)}) collective-permute-start(bf16[3,3072,384]{2,1,0:T(8,128)(2,1)} %bitcast.4), channel_id=1, source_target_pairs={{0,16},{16,0},{1,17},{17,1},{2,18},{18,2},{3,19},{19,3},{4,20},{20... | collective-permute-start | bytes 21233672 | tf_op jit(solution)/shard_map/ppermute | solution.py:248
  1.1 9.5 %collective-permute-start.2 = (bf16[512,384]{1,0:T(8,128)(2,1)S(1)}, bf16[512,384]{1,0:T(8,128)(2,1)S(1)}, u32[]{:S(2)}, u32[]{:S(2)}) collective-permute-start(bf16[512,384]{1,0:T(8,128)(2,1)S(1)} %get-tuple-element.15.refs_0_.refs_4_), channel_id=1, source_target_pairs={{0,2},{1,3},{2,0},{3,1},{4,6},{5,7},{6,4},{7,5},{8,10},{9,11},{10,... | collective-permute-start | bytes 1179656 | tf_op jit(solution)/shard_map/ppermute | solution.py:31
  4.3 10.5 %collective-permute-start = (bf16[512,384]{1,0:T(8,128)(2,1)}, bf16[512,384]{1,0:T(8,128)(2,1)S(1)}, u32[]{:S(2)}, u32[]{:S(2)}) collective-permute-start(bf16[512,384]{1,0:T(8,128)(2,1)} %bitcast.8), channel_id=1, source_target_pairs={{0,1},{1,2},{2,3},{3,0},{4,5},{5,6},{6,7},{7,4},{8,9},{9,10},{10,1... | collective-permute-start | bytes 1179656 | tf_op jit(solution)/shard_map/ppermute | solution.py:31
  4.8 10.0 %collective-permute-start.1 = (bf16[512,384]{1,0:T(8,128)(2,1)}, bf16[512,384]{1,0:T(8,128)(2,1)S(1)}, u32[]{:S(2)}, u32[]{:S(2)}) collective-permute-start(bf16[512,384]{1,0:T(8,128)(2,1)} %bitcast.9), channel_id=1, source_target_pairs={{0,3},{1,0},{2,1},{3,2},{4,7},{5,4},{6,5},{7,6},{8,11},{9,8},{10,9... | collective-permute-start | bytes 1179656 | tf_op jit(solution)/shard_map/ppermute | solution.py:31
  14.9 12.1 %collective-permute-start.6 = (bf16[4,256,384]{2,1,0:T(8,128)(2,1)S(1)}, bf16[4,256,384]{2,1,0:T(8,128)(2,1)S(1)}, u32[]{:S(2)}, u32[]{:S(2)}) collective-permute-start(bf16[4,256,384]{2,1,0:T(8,128)(2,1)S(1)} %shard_map.38.refs_2_.refs_0_), channel_id=1, source_target_pairs={{0,4},{1,5},{2,6},{3,7},{4,8},{5,9},{6,10},{7,11},{8,12},{9,13},{1... | collective-permute-start | bytes 2359304 | tf_op jit(solution)/shard_map/ppermute | solution.py:31
  16.8 13.2 %collective-permute-start.7 = (bf16[4,256,384]{2,1,0:T(8,128)(2,1)S(1)}, bf16[4,256,384]{2,1,0:T(8,128)(2,1)S(1)}, u32[]{:S(2)}, u32[]{:S(2)}) collective-permute-start(bf16[4,256,384]{2,1,0:T(8,128)(2,1)S(1)} %shard_map.38.refs_2_.refs_0_), channel_id=1, source_target_pairs={{0,12},{1,13},{2,14},{3,15},{4,0},{5,1},{6,2},{7,3},{8,4},{9,5},{1... | collective-permute-start | bytes 2359304 | tf_op jit(solution)/shard_map/ppermute | solution.py:31
  21.4 14.0 %collective-permute-start.4 = (bf16[4,256,384]{2,1,0:T(8,128)(2,1)S(1)}, bf16[4,256,384]{2,1,0:T(8,128)(2,1)S(1)}, u32[]{:S(2)}, u32[]{:S(2)}) collective-permute-start(bf16[4,256,384]{2,1,0:T(8,128)(2,1)S(1)} %shard_map.40.refs_2_.refs_0_), channel_id=1, source_target_pairs={{0,4},{1,5},{2,6},{3,7},{4,8},{5,9},{6,10},{7,11},{8,12},{9,13},{1... | collective-permute-start | bytes 2359304 | tf_op jit(solution)/shard_map/ppermute | solution.py:31
  23.8 14.7 %collective-permute-start.5 = (bf16[4,256,384]{2,1,0:T(8,128)(2,1)S(1)}, bf16[4,256,384]{2,1,0:T(8,128)(2,1)S(1)}, u32[]{:S(2)}, u32[]{:S(2)}) collective-permute-start(bf16[4,256,384]{2,1,0:T(8,128)(2,1)S(1)} %shard_map.40.refs_2_.refs_0_), channel_id=1, source_target_pairs={{0,12},{1,13},{2,14},{3,15},{4,0},{5,1},{6,2},{7,3},{8,4},{9,5},{1... | collective-permute-start | bytes 2359304 | tf_op jit(solution)/shard_map/ppermute | solution.py:31
  30.1 10.5 %collective-permute-start.10 = (bf16[2,256,384]{2,1,0:T(8,128)(2,1)S(1)}, bf16[2,256,384]{2,1,0:T(8,128)(2,1)S(1)}, u32[]{:S(2)}, u32[]{:S(2)}) collective-permute-start(bf16[2,256,384]{2,1,0:T(8,128)(2,1)S(1)} %get-tuple-element.16.refs_4_), channel_id=1, source_target_pairs={{0,4},{1,5},{2,6},{3,7},{4,8},{5,9},{6,10},{7,11},{8,12},{9,13},{1... | collective-permute-start | bytes 1179656 | tf_op jit(solution)/shard_map/ppermute | solution.py:31
  30.2 12.5 %collective-permute-start.11 = (bf16[2,256,384]{2,1,0:T(8,128)(2,1)S(1)}, bf16[2,256,384]{2,1,0:T(8,128)(2,1)S(1)}, u32[]{:S(2)}, u32[]{:S(2)}) collective-permute-start(bf16[2,256,384]{2,1,0:T(8,128)(2,1)S(1)} %get-tuple-element.19), channel_id=1, source_target_pairs={{0,12},{1,13},{2,14},{3,15},{4,0},{5,1},{6,2},{7,3},{8,4},{9,5},{1... | collective-permute-start | bytes 1179656 | tf_op jit(solution)/shard_map/ppermute | solution.py:31
  38.5 7.9 %collective-permute-start.8 = (bf16[2,256,384]{2,1,0:T(8,128)(2,1)S(1)}, bf16[2,256,384]{2,1,0:T(8,128)(2,1)S(1)}, u32[]{:S(2)}, u32[]{:S(2)}) collective-permute-start(bf16[2,256,384]{2,1,0:T(8,128)(2,1)S(1)} %get-tuple-element.17.refs_6_), channel_id=1, source_target_pairs={{0,4},{1,5},{2,6},{3,7},{4,8},{5,9},{6,10},{7,11},{8,12},{9,13},{1... | collective-permute-start | bytes 1179656 | tf_op jit(solution)/shard_map/ppermute | solution.py:31
  38.6 9.1 %collective-permute-start.9 = (bf16[2,256,384]{2,1,0:T(8,128)(2,1)S(1)}, bf16[2,256,384]{2,1,0:T(8,128)(2,1)S(1)}, u32[]{:S(2)}, u32[]{:S(2)}) collective-permute-start(bf16[2,256,384]{2,1,0:T(8,128)(2,1)S(1)} %get-tuple-element.18), channel_id=1, source_target_pairs={{0,12},{1,13},{2,14},{3,15},{4,0},{5,1},{6,2},{7,3},{8,4},{9,5},{1... | collective-permute-start | bytes 1179656 | tf_op jit(solution)/shard_map/ppermute | solution.py:31
  43.9 7.9 %collective-permute-start.13 = (bf16[256,384]{1,0:T(8,128)(2,1)S(1)}, bf16[256,384]{1,0:T(8,128)(2,1)S(1)}, u32[]{:S(2)}, u32[]{:S(2)}) collective-permute-start(bf16[256,384]{1,0:T(8,128)(2,1)S(1)} %shard_map.46.refs_4_), channel_id=1, source_target_pairs={{0,32},{32,64},{64,96},{96,128},{128,160},{160,192},{192,224},{224... | collective-permute-start | bytes 589832 | tf_op jit(solution)/shard_map/ppermute | solution.py:36
  48.9 8.2 %collective-permute-start.12 = (bf16[256,384]{1,0:T(8,128)(2,1)S(1)}, bf16[256,384]{1,0:T(8,128)(2,1)S(1)}, u32[]{:S(2)}, u32[]{:S(2)}) collective-permute-start(bf16[256,384]{1,0:T(8,128)(2,1)S(1)} %shard_map.48.refs_1_), channel_id=1, source_target_pairs={{0,32},{32,64},{64,96},{96,128},{128,160},{160,192},{192,224},{224... | collective-permute-start | bytes 589832 | tf_op jit(solution)/shard_map/ppermute | solution.py:36
  51.9 8.6 %collective-permute-start.17 = (bf16[256,384]{1,0:T(8,128)(2,1)S(1)}, bf16[256,384]{1,0:T(8,128)(2,1)S(1)}, u32[]{:S(2)}, u32[]{:S(2)}) collective-permute-start(bf16[256,384]{1,0:T(8,128)(2,1)S(1)} %shard_map.49.refs_1_.refs_0_.refs_4_), channel_id=1, source_target_pairs={{0,1},{1,2},{2,3},{3,0},{4,5},{5,6},{6,7},{7,4},{8,9},{9,10},{10,1... | collective-permute-start | bytes 589832 | tf_op jit(solution)/shard_map/ppermute | solution.py:31
  53.7 7.8 %collective-permute-start.18 = (bf16[256,384]{1,0:T(8,128)(2,1)S(1)}, bf16[256,384]{1,0:T(8,128)(2,1)S(1)}, u32[]{:S(2)}, u32[]{:S(2)}) collective-permute-start(bf16[256,384]{1,0:T(8,128)(2,1)S(1)} %shard_map.49.refs_1_.refs_0_.refs_4_), channel_id=1, source_target_pairs={{0,3},{1,0},{2,1},{3,2},{4,7},{5,4},{6,5},{7,6},{8,11},{9,8},{10,9... | collective-permute-start | bytes 589832 | tf_op jit(solution)/shard_map/ppermute | solution.py:31
  55.2 7.2 %collective-permute-start.19 = (bf16[256,384]{1,0:T(8,128)(2,1)S(1)}, bf16[256,384]{1,0:T(8,128)(2,1)S(1)}, u32[]{:S(2)}, u32[]{:S(2)}) collective-permute-start(bf16[256,384]{1,0:T(8,128)(2,1)S(1)} %shard_map.49.refs_1_.refs_0_.refs_4_), channel_id=1, source_target_pairs={{0,2},{1,3},{2,0},{3,1},{4,6},{5,7},{6,4},{7,5},{8,10},{9,11},{10,... | collective-permute-start | bytes 589832 | tf_op jit(solution)/shard_map/ppermute | solution.py:31
  57.1 9.2 %collective-permute-start.14 = (bf16[256,384]{1,0:T(8,128)(2,1)S(1)}, bf16[256,384]{1,0:T(8,128)(2,1)S(1)}, u32[]{:S(2)}, u32[]{:S(2)}) collective-permute-start(bf16[256,384]{1,0:T(8,128)(2,1)S(1)} %shard_map.50.refs_4_.refs_0_), channel_id=1, source_target_pairs={{0,1},{1,2},{2,3},{3,0},{4,5},{5,6},{6,7},{7,4},{8,9},{9,10},{10,1... | collective-permute-start | bytes 589832 | tf_op jit(solution)/shard_map/ppermute | solution.py:31
  58.7 7.8 %collective-permute-start.15 = (bf16[256,384]{1,0:T(8,128)(2,1)S(1)}, bf16[256,384]{1,0:T(8,128)(2,1)S(1)}, u32[]{:S(2)}, u32[]{:S(2)}) collective-permute-start(bf16[256,384]{1,0:T(8,128)(2,1)S(1)} %shard_map.50.refs_4_.refs_0_), channel_id=1, source_target_pairs={{0,3},{1,0},{2,1},{3,2},{4,7},{5,4},{6,5},{7,6},{8,11},{9,8},{10,9... | collective-permute-start | bytes 589832 | tf_op jit(solution)/shard_map/ppermute | solution.py:31
  60.5 9.8 %collective-permute-start.16 = (bf16[256,384]{1,0:T(8,128)(2,1)S(1)}, bf16[256,384]{1,0:T(8,128)(2,1)S(1)}, u32[]{:S(2)}, u32[]{:S(2)}) collective-permute-start(bf16[256,384]{1,0:T(8,128)(2,1)S(1)} %shard_map.50.refs_4_.refs_0_), channel_id=1, source_target_pairs={{0,2},{1,3},{2,0},{3,1},{4,6},{5,7},{6,4},{7,5},{8,10},{9,11},{10,... | collective-permute-start | bytes 589832 | tf_op jit(solution)/shard_map/ppermute | solution.py:31
  62.5 12.3 %collective-permute-start.22 = (bf16[4,256,384]{2,1,0:T(8,128)(2,1)S(1)}, bf16[4,256,384]{2,1,0:T(8,128)(2,1)S(1)}, u32[]{:S(2)}, u32[]{:S(2)}) collective-permute-start(bf16[4,256,384]{2,1,0:T(8,128)(2,1)S(1)} %shard_map.51.refs_4_.refs_0_), channel_id=1, source_target_pairs={{0,4},{1,5},{2,6},{3,7},{4,8},{5,9},{6,10},{7,11},{8,12},{9,13},{1... | collective-permute-start | bytes 2359304 | tf_op jit(solution)/shard_map/ppermute | solution.py:31
  63.2 13.2 %collective-permute-start.23 = (bf16[4,256,384]{2,1,0:T(8,128)(2,1)S(1)}, bf16[4,256,384]{2,1,0:T(8,128)(2,1)S(1)}, u32[]{:S(2)}, u32[]{:S(2)}) collective-permute-start(bf16[4,256,384]{2,1,0:T(8,128)(2,1)S(1)} %shard_map.51.refs_4_.refs_0_), channel_id=1, source_target_pairs={{0,12},{1,13},{2,14},{3,15},{4,0},{5,1},{6,2},{7,3},{8,4},{9,5},{1... | collective-permute-start | bytes 2359304 | tf_op jit(solution)/shard_map/ppermute | solution.py:31
  70.3 12.9 %collective-permute-start.20 = (bf16[4,256,384]{2,1,0:T(8,128)(2,1)S(1)}, bf16[4,256,384]{2,1,0:T(8,128)(2,1)S(1)}, u32[]{:S(2)}, u32[]{:S(2)}) collective-permute-start(bf16[4,256,384]{2,1,0:T(8,128)(2,1)S(1)} %shard_map.52.refs_2_.refs_0_), channel_id=1, source_target_pairs={{0,4},{1,5},{2,6},{3,7},{4,8},{5,9},{6,10},{7,11},{8,12},{9,13},{1... | collective-permute-start | bytes 2359304 | tf_op jit(solution)/shard_map/ppermute | solution.py:31
  70.4 14.4 %collective-permute-start.21 = (bf16[4,256,384]{2,1,0:T(8,128)(2,1)S(1)}, bf16[4,256,384]{2,1,0:T(8,128)(2,1)S(1)}, u32[]{:S(2)}, u32[]{:S(2)}) collective-permute-start(bf16[4,256,384]{2,1,0:T(8,128)(2,1)S(1)} %shard_map.52.refs_2_.refs_0_), channel_id=1, source_target_pairs={{0,12},{1,13},{2,14},{3,15},{4,0},{5,1},{6,2},{7,3},{8,4},{9,5},{1... | collective-permute-start | bytes 2359304 | tf_op jit(solution)/shard_map/ppermute | solution.py:31
  76.5 10.9 %collective-permute-start.26 = (bf16[2,256,384]{2,1,0:T(8,128)(2,1)S(1)}, bf16[2,256,384]{2,1,0:T(8,128)(2,1)S(1)}, u32[]{:S(2)}, u32[]{:S(2)}) collective-permute-start(bf16[2,256,384]{2,1,0:T(8,128)(2,1)S(1)} %get-tuple-element.21.refs_4_), channel_id=1, source_target_pairs={{0,4},{1,5},{2,6},{3,7},{4,8},{5,9},{6,10},{7,11},{8,12},{9,13},{1... | collective-permute-start | bytes 1179656 | tf_op jit(solution)/shard_map/ppermute | solution.py:31
  76.9 12.2 %collective-permute-start.27 = (bf16[2,256,384]{2,1,0:T(8,128)(2,1)S(1)}, bf16[2,256,384]{2,1,0:T(8,128)(2,1)S(1)}, u32[]{:S(2)}, u32[]{:S(2)}) collective-permute-start(bf16[2,256,384]{2,1,0:T(8,128)(2,1)S(1)} %get-tuple-element.24), channel_id=1, source_target_pairs={{0,12},{1,13},{2,14},{3,15},{4,0},{5,1},{6,2},{7,3},{8,4},{9,5},{1... | collective-permute-start | bytes 1179656 | tf_op jit(solution)/shard_map/ppermute | solution.py:31
  84.9 7.9 %collective-permute-start.24 = (bf16[2,256,384]{2,1,0:T(8,128)(2,1)S(1)}, bf16[2,256,384]{2,1,0:T(8,128)(2,1)S(1)}, u32[]{:S(2)}, u32[]{:S(2)}) collective-permute-start(bf16[2,256,384]{2,1,0:T(8,128)(2,1)S(1)} %get-tuple-element.22.refs_5_), channel_id=1, source_target_pairs={{0,4},{1,5},{2,6},{3,7},{4,8},{5,9},{6,10},{7,11},{8,12},{9,13},{1... | collective-permute-start | bytes 1179656 | tf_op jit(solution)/shard_map/ppermute | solution.py:31
  85.3 9.0 %collective-permute-start.25 = (bf16[2,256,384]{2,1,0:T(8,128)(2,1)S(1)}, bf16[2,256,384]{2,1,0:T(8,128)(2,1)S(1)}, u32[]{:S(2)}, u32[]{:S(2)}) collective-permute-start(bf16[2,256,384]{2,1,0:T(8,128)(2,1)S(1)} %get-tuple-element.23), channel_id=1, source_target_pairs={{0,12},{1,13},{2,14},{3,15},{4,0},{5,1},{6,2},{7,3},{8,4},{9,5},{1... | collective-permute-start | bytes 1179656 | tf_op jit(solution)/shard_map/ppermute | solution.py:31

commit v3 on v2

v3 whole, which is shorter than its diff:
```python
import functools

import jax
import jax.numpy as jnp
from jax import lax
from jax.experimental import pallas as pl
from jax.experimental.pallas import tpu as pltpu
from jax.sharding import PartitionSpec as P

SIDE = 4
PLANE = ("row", "col")
NEAR = (0, -1, 1, 2)
HALF = 256
VMEM = pl.BlockSpec(memory_space=pltpu.VMEM)
ANY = pl.BlockSpec(memory_space=pl.ANY)


def ring_pairs(step, first):
    pairs = []
    for core in range(2):
        for col in range(SIDE * SIDE):
            y, x = divmod(col, SIDE)
            if (core == 0) == first:
                x = (x + step) % SIDE
            else:
                y = (y + step) % SIDE
            pairs.append((core * SIDE * SIDE + col, core * SIDE * SIDE + y * SIDE + x))
    return pairs


def shift(value, step, first):
    return lax.ppermute(value, PLANE, ring_pairs(step, first))


def relay(output):
    count = lax.axis_size("section")
    return lax.ppermute(output, "section", [(s, (s + 1) % count) for s in range(count)])


def block_ids():
    core, col = lax.axis_index("row"), lax.axis_index("col")
    y, x = col // SIDE, col % SIDE
    ids = []
    for second in NEAR:
        for first in NEAR:
            along_x = first + core * (second - first)
            along_y = second + core * (first - second)
            block = (y + along_y + SIDE) % SIDE * SIDE + (x + along_x + SIDE) % SIDE
            ids.append(((block // 8 + core) % 2, block % 8))
    return ids


def in_vmem(value):
    return pltpu.with_memory_space_constraint(value, pltpu.VMEM)


def in_hbm(value):
    return pltpu.with_memory_space_constraint(value, pltpu.HBM)


def run(kernel, out_shape, operands, after=(), specs=None, scratch=(), megabytes=4, place=VMEM):
    operands = list(operands)
    if specs is None:
        specs = [VMEM] * len(operands)
        operands = [in_vmem(v) for v in operands]
    count = len(operands)

    def body(*refs):
        kernel(*refs[:count], *refs[count + len(after) :])

    return pl.pallas_call(
        body,
        out_shape=out_shape,
        in_specs=specs + [VMEM] * len(after),
        out_specs=jax.tree.map(lambda _: place, out_shape),
        scratch_shapes=list(scratch),
        compiler_params=pltpu.CompilerParams(vmem_limit_bytes=megabytes * 1024 * 1024),
        cost_estimate=pl.CostEstimate(flops=1, bytes_accessed=1, transcendentals=0),
    )(*operands, *map(in_vmem, after))


def arrange(own, other, after):
    _, half, width = own.shape
    depth = half // 8

    def kernel(own, other, out, sems):
        ids = block_ids()

        def copy(source, block, k):
            rows = pl.ds(pl.multiple_of(ids[block][1] * depth, depth), depth)
            place = out.at[pl.ds(block * depth, depth), pl.ds(k * width, width)]
            return pltpu.make_async_copy(source.at[k, rows, :], place, sems.at[block, k])

        for block in range(SIDE * SIDE):

            @pl.when(ids[block][0] == 0)
            def _():
                for k in range(3):
                    copy(own, block, k).start()

            @pl.when(ids[block][0] != 0)
            def _():
                for k in range(3):
                    copy(other, block, k).start()

        for block in range(SIDE * SIDE):
            for k in range(3):
                copy(own, block, k).wait()

    return run(
        kernel,
        pltpu.VMEM((2 * half, 3 * width), jnp.bfloat16),
        [in_hbm(own), in_vmem(other)],
        after,
        specs=[ANY, VMEM],
        scratch=[pltpu.SemaphoreType.DMA((SIDE * SIDE, 3))],
    )


def bring_in(values):
    def kernel(*refs):
        sems = refs[-1]
        count = len(values)
        copies = [
            pltpu.make_async_copy(refs[i], refs[count + i], sems.at[i]) for i in range(count)
        ]
        for copy in copies:
            copy.start()
        for copy in copies:
            copy.wait()

    return run(
        kernel,
        tuple(pltpu.VMEM(v.shape, v.dtype) for v in values),
        [in_hbm(v) for v in values],
        specs=[ANY] * len(values),
        scratch=[pltpu.SemaphoreType.DMA((len(values),))],
    )


def stack(pieces, after):
    arrays, picks = operands_of(pieces)

    def kernel(*refs):
        for i, (n, what) in enumerate(picks):
            refs[-1][i] = refs[n][what]

    kind = pltpu.VMEM((len(pieces), HALF, arrays[0].shape[-1]), jnp.bfloat16)
    return run(kernel, kind, arrays, after)


def operands_of(pieces):
    arrays, picks = [], []
    for array, what in pieces:
        known = [n for n, other in enumerate(arrays) if other is array]
        if not known:
            arrays.append(array)
        picks.append((known[0] if known else len(arrays) - 1, what))
    return arrays, picks


def same(value, after):
    def kernel(value, out):
        out[...] = value[...]

    return run(kernel, pltpu.VMEM(value.shape, value.dtype), [value], after)


def products(refs, picks, weights, first):
    acts = jnp.concatenate([refs[n][what] for n, what in picks], axis=1)
    start = first * refs[0].shape[-1]
    return jnp.dot(acts, weights[start : start + acts.shape[1]], preferred_element_type=jnp.float32)


def partial(pieces, first, weights, acc, after):
    arrays, picks = operands_of(pieces)

    def kernel(*refs):
        value = products(refs, picks, refs[len(arrays)], first)
        refs[-1][...] = value if acc is None else refs[len(arrays) + 1][...] + value

    kind = pltpu.VMEM((HALF, 3 * arrays[0].shape[-1]), jnp.float32)
    operands = [*arrays, weights] + ([] if acc is None else [acc])
    return run(kernel, kind, operands, after, megabytes=16)


def finish(far, weights, acc, own, injected, before, after):
    arrays, picks = operands_of([(part, i) for part in far for i in range(2)])
    width = arrays[0].shape[-1]
    operands = [in_vmem(v) for v in (*arrays, weights, acc, own[0])]
    specs = [VMEM] * len(operands)
    scratch = []
    if injected is not None:
        operands.append(in_vmem(injected[0]))
        specs.append(VMEM)
    if before is not None:
        operands.append(in_vmem(before))
        specs.append(VMEM)
    if before is not None:
        scratch = [pltpu.VMEM((HALF, width), jnp.bfloat16), pltpu.SemaphoreType.DMA((2,))]

    def kernel(*refs):
        weights, acc, acts = refs[len(arrays) : len(arrays) + 3]
        out = refs[len(operands)]
        if scratch:
            kept, sems = refs[-2:]
        if before is not None:
            store = pltpu.make_async_copy(refs[len(operands) - 1], out.at[pl.ds(0, HALF)], sems.at[0])
            store.start()
        total = acc[...] + products(refs, picks, weights, 3 * SIDE)
        first, second, third = (total[:, k * width : (k + 1) * width] for k in range(3))
        gate = 1.0 / (1.0 + jnp.exp(-third))
        cubic = 0.7978845608 * (first + 0.044715 * (first * first * first))
        value = acts[own[1]].astype(jnp.float32)
        value += gate * (0.5 * first * (1.0 + jnp.tanh(cubic))) * second
        value = value.astype(jnp.bfloat16)
        if injected is not None:
            last = lax.axis_index("section") == lax.axis_size("section") - 1
            value = jnp.where(last, refs[len(operands) - 1][injected[1]], value)
        if before is None:
            out[...] = value
        else:
            kept[...] = value
            rest = pltpu.make_async_copy(kept, out.at[pl.ds(HALF, HALF)], sems.at[1])
            rest.start()
            store.wait()
            rest.wait()

    if before is None:
        kind, place = pltpu.VMEM((HALF, width), jnp.bfloat16), VMEM
    else:
        kind, place = jax.ShapeDtypeStruct((2 * HALF, width), jnp.bfloat16), ANY
    return run(kernel, kind, operands, after, specs=specs, scratch=scratch, megabytes=16, place=place)


def first_phase(acts):
    return [acts] + [shift(acts, step, True) for step in (1, 3, 2)]


def both_ways(value):
    return shift(value, 1, False), shift(value, 3, False)


def third_phase(up, down, after):
    arrays, picks = operands_of(up[:2] + down[2:])

    def kernel(*refs):
        for i, (n, what) in enumerate(picks):
            refs[len(arrays) + i // 2][i % 2] = refs[n][what]

    kind = pltpu.VMEM((2, HALF, arrays[0].shape[-1]), jnp.bfloat16)
    one, two = run(kernel, (kind, kind), arrays, after)
    return (shift(one, 1, False), shift(two, 3, False)), one


def body(in_flight, injected, weights):
    own = weights[0]
    other = lax.ppermute(own, "row", [(0, 1), (1, 0)])
    low, high = slice(0, HALF), slice(HALF, 2 * HALF)
    every = slice(0, HALF)

    near = [shift(in_flight[0], step, True) for step in (1, 3)]
    acts, injected = bring_in([in_flight[0], injected[0]])
    near = [*near, shift(acts, 2, True)]
    near_a = stack([(block, low) for block in [acts, *near]], [])
    up, down = both_ways(near_a)
    up_a = [(up, i) for i in range(SIDE)]
    down_a = [(down, i) for i in range(SIDE)]
    near_a = [(near_a, i) for i in range(SIDE)]
    arranged = arrange(own, other, [near_a[0][0]])
    near_b = stack([(block, high) for block in [acts, *near]], [arranged])
    up, down = both_ways(near_b)
    up_b = [(up, i) for i in range(SIDE)]
    down_b = [(down, i) for i in range(SIDE)]
    near_b = [(near_b, i) for i in range(SIDE)]
    acc_a = partial(near_a, 0, arranged, None, [near_b[0][0]])
    acc_b = partial(near_b, 0, arranged, None, [acc_a])
    far_a, sent = third_phase(up_a, down_a, [acc_b])
    acc_a = partial(up_a + down_a, SIDE, arranged, acc_a, [sent])
    far_b, sent = third_phase(up_b, down_b, [acc_a])
    out_a = finish(far_a, arranged, acc_a, near_a[0], (injected, low), None, [sent])
    acc_b = partial(up_b + down_b, SIDE, arranged, acc_b, [out_a])
    out_b = finish(far_b, arranged, acc_b, near_b[0], (injected, high), None, [])

    acts_a = relay(out_a)
    acts_b = relay(out_b)
    near_a = stack([(block, every) for block in first_phase(acts_a)], [acts_b])
    up, down = both_ways(near_a)
    up_a = [(up, i) for i in range(SIDE)]
    down_a = [(down, i) for i in range(SIDE)]
    near_a = [(near_a, i) for i in range(SIDE)]
    near_b = stack([(block, every) for block in first_phase(acts_b)], [near_a[0][0]])
    up, down = both_ways(near_b)
    up_b = [(up, i) for i in range(SIDE)]
    down_b = [(down, i) for i in range(SIDE)]
    near_b = [(near_b, i) for i in range(SIDE)]
    acc_a = partial(near_a, 0, arranged, None, [near_b[0][0]])
    acc_b = partial(near_b, 0, arranged, None, [acc_a])
    far_a, sent = third_phase(up_a, down_a, [acc_b])
    acc_a = partial(up_a + down_a, SIDE, arranged, acc_a, [sent])
    far_b, sent = third_phase(up_b, down_b, [acc_a])
    out_a = finish(far_a, arranged, acc_a, near_a[0], None, None, [sent])
    acc_b = partial(up_b + down_b, SIDE, arranged, acc_b, [out_a])
    return finish(far_b, arranged, acc_b, near_b[0], None, out_a, [])[None]


def solution(mesh):
    placed = (P("section", "row", "col"), P(None, "row", "col"), P("section", None, "row", "col"))
    return jax.shard_map(
        body, mesh=mesh, in_specs=placed, out_specs=P("section", "row", "col"), check_vma=False
    )
```

time: 96.3 us -> 96.4 us (level)
    pallas_call x24 -> x22, Pallas kernels: 25.1 us -> 25 us  [run(): pl.pallas_call(body, out_shape=out_shape, in_specs=specs + [VMEM] * len(a...]
where the time goes in v3:
time: 96.4 us; the launch traced here: 96.3 us
  waiting for transfers between devices  37.1 us (38%)
  starting transfers between devices  33.8 us (35%)
  Pallas kernels  25 us (26%)
    ppermute x25, waiting for transfers between devices, shift(): return lax.ppermute(value, PLANE, ring_pairs(step, first))  34.3 us
    ppermute x25, starting transfers between devices, shift(): return lax.ppermute(value, PLANE, ring_pairs(step, first))  32.6 us
    pallas_call x22, Pallas kernels, run(): pl.pallas_call(body, out_shape=out_shape, in_specs=specs + [VMEM] * len(a...  25 us
    ppermute x2, waiting for transfers between devices, relay(): lax.ppermute(output, 'section', [(s, (s + 1) % count) for s in range(coun...  2.79 us
  transfers between devices with their start and end apart: 28, of which 22 were waited for; matrix products, arithmetic and copies ran while one was open for 0% of the time, Pallas kernels for 24%

profile of v3, /device:TPU:24, one launch (start us, length us, event | category | flops | bytes accessed | tf_op | source)
XLA Modules:
  0.0 96.3 jit_solution(11123230767749465102)
XLA Ops:
  1.1 3.1 %collective-permute-start.2 = (bf16[512,384]{1,0:T(8,128)(2,1)S(1)}, bf16[512,384]{1,0:T(8,128)(2,1)S(1)}, u32[]{:S(2)}, u32[]{:S(2)}) collective-permute-start(bf16[512,384]{1,0:T(8,128)(2,1)S(1)} %get-tuple-element.15.refs_0_), channel_id=1, source_target_pairs={{0,2},{1,3},{2,0},{3,1},{4,6},{5,7},{6,4},{7,5},{8,10},{9,11},{10,... | collective-permute-start | bytes 1179656 | tf_op jit(solution)/shard_map/ppermute | solution.py:32
  4.8 2.6 %collective-permute-start.1 = (bf16[512,384]{1,0:T(8,128)(2,1)}, bf16[512,384]{1,0:T(8,128)(2,1)S(1)}, u32[]{:S(2)}, u32[]{:S(2)}) collective-permute-start(bf16[512,384]{1,0:T(8,128)(2,1)} %bitcast.9), channel_id=1, source_target_pairs={{0,3},{1,0},{2,1},{3,2},{4,7},{5,4},{6,5},{7,6},{8,11},{9,8},{10,9... | collective-permute-start | bytes 1179656 | tf_op jit(solution)/shard_map/ppermute | solution.py:32
  7.5 3.1 %collective-permute-done.2.refs_3_ = bf16[512,384]{1,0:T(8,128)(2,1)S(1)} collective-permute-done((bf16[512,384]{1,0:T(8,128)(2,1)S(1)}, bf16[512,384]{1,0:T(8,128)(2,1)S(1)}, u32[]{:S(2)}, u32[]{:S(2)}) %collective-permute-start.2) | collective-permute-done | bytes 393248 | tf_op jit(solution)/shard_map/ppermute | solution.py:32
  10.6 4.1 %collective-permute-done.refs_1_ = bf16[512,384]{1,0:T(8,128)(2,1)S(1)} collective-permute-done((bf16[512,384]{1,0:T(8,128)(2,1)}, bf16[512,384]{1,0:T(8,128)(2,1)S(1)}, u32[]{:S(2)}, u32[]{:S(2)}) %collective-permute-start) | collective-permute-done | bytes 393248 | tf_op jit(solution)/shard_map/ppermute | solution.py:32
  14.9 2.0 %collective-permute-start.6 = (bf16[4,256,384]{2,1,0:T(8,128)(2,1)S(1)}, bf16[4,256,384]{2,1,0:T(8,128)(2,1)S(1)}, u32[]{:S(2)}, u32[]{:S(2)}) collective-permute-start(bf16[4,256,384]{2,1,0:T(8,128)(2,1)S(1)} %shard_map.38.refs_2_.refs_0_.refs_4_), channel_id=1, source_target_pairs={{0,4},{1,5},{2,6},{3,7},{4,8},{5,9},{6,10},{7,11},{8,12},{9,13},{1... | collective-permute-start | bytes 2359304 | tf_op jit(solution)/shard_map/ppermute | solution.py:32
  17.0 4.3 %shard_map.39.refs_4_.refs_1_.refs_2_ = bf16[6144,1152]{1,0:T(8,128)(2,1)S(1)} custom-call(bf16[3,3072,384]{2,1,0:T(8,128)(2,1)} %bitcast.5, bf16[3,3072,384]{2,1,0:T(8,128)(2,1)S(1)} %collective-permute-done.3.refs_1_, bf16[4,256,384]{2,1,0:T(8,128)(2,1)S(1)} %shard_map.38.refs_2_.refs_0_.refs_4_), custom_call_target="tpu_custom_call" | custom-call | flops 1 | bytes 1 | tf_op jit(solution)/shard_map/pallas_call | solution.py:71
  21.4 2.4 %collective-permute-start.4 = (bf16[4,256,384]{2,1,0:T(8,128)(2,1)S(1)}, bf16[4,256,384]{2,1,0:T(8,128)(2,1)S(1)}, u32[]{:S(2)}, u32[]{:S(2)}) collective-permute-start(bf16[4,256,384]{2,1,0:T(8,128)(2,1)S(1)} %shard_map.40.refs_2_.refs_0_.refs_4_), channel_id=1, source_target_pairs={{0,4},{1,5},{2,6},{3,7},{4,8},{5,9},{6,10},{7,11},{8,12},{9,13},{1... | collective-permute-start | bytes 2359304 | tf_op jit(solution)/shard_map/ppermute | solution.py:32
  26.9 3.1 %collective-permute-done.7.refs_1_ = bf16[4,256,384]{2,1,0:T(8,128)(2,1)S(1)} collective-permute-done((bf16[4,256,384]{2,1,0:T(8,128)(2,1)S(1)}, bf16[4,256,384]{2,1,0:T(8,128)(2,1)S(1)}, u32[]{:S(2)}, u32[]{:S(2)}) %collective-permute-start.7) | collective-permute-done | bytes 786464 | tf_op jit(solution)/shard_map/ppermute | solution.py:32
  30.2 2.0 %collective-permute-start.11 = (bf16[2,256,384]{2,1,0:T(8,128)(2,1)S(1)}, bf16[2,256,384]{2,1,0:T(8,128)(2,1)S(1)}, u32[]{:S(2)}, u32[]{:S(2)}) collective-permute-start(bf16[2,256,384]{2,1,0:T(8,128)(2,1)S(1)} %get-tuple-element.19), channel_id=1, source_target_pairs={{0,12},{1,13},{2,14},{3,15},{4,0},{5,1},{6,2},{7,3},{8,4},{9,5},{1... | collective-permute-start | bytes 1179656 | tf_op jit(solution)/shard_map/ppermute | solution.py:32
  32.2 2.2 %shard_map.44.refs_2_.refs_3_ = f32[256,1152]{1,0:T(8,128)S(1)} custom-call(bf16[4,256,384]{2,1,0:T(8,128)(2,1)S(1)} %collective-permute-done.6.refs_0_, bf16[4,256,384]{2,1,0:T(8,128)(2,1)S(1)} %collective-permute-done.7.refs_1_, bf16[6144,1152]{1,0:T(8,128)(2,1)S(1)} %shard_map.39.refs_4_.refs_1_.refs_2_, f32[256,1152]{1,0:T(8,128)S(1)} %shard_map.41.refs_2_.refs_3_, ...), custom_call_target="tpu_custom_call" | custom-call | flops 1 | bytes 1 | tf_op jit(solution)/shard_map/pallas_call | solution.py:71
  35.4 3.1 %collective-permute-done.5.refs_1_ = bf16[4,256,384]{2,1,0:T(8,128)(2,1)S(1)} collective-permute-done((bf16[4,256,384]{2,1,0:T(8,128)(2,1)S(1)}, bf16[4,256,384]{2,1,0:T(8,128)(2,1)S(1)}, u32[]{:S(2)}, u32[]{:S(2)}) %collective-permute-start.5) | collective-permute-done | bytes 786464 | tf_op jit(solution)/shard_map/ppermute | solution.py:32
  38.6 2.0 %collective-permute-start.9 = (bf16[2,256,384]{2,1,0:T(8,128)(2,1)S(1)}, bf16[2,256,384]{2,1,0:T(8,128)(2,1)S(1)}, u32[]{:S(2)}, u32[]{:S(2)}) collective-permute-start(bf16[2,256,384]{2,1,0:T(8,128)(2,1)S(1)} %get-tuple-element.18), channel_id=1, source_target_pairs={{0,12},{1,13},{2,14},{3,15},{4,0},{5,1},{6,2},{7,3},{8,4},{9,5},{1... | collective-permute-start | bytes 1179656 | tf_op jit(solution)/shard_map/ppermute | solution.py:32
  40.6 2.0 %collective-permute-done.11.refs_1_ = bf16[2,256,384]{2,1,0:T(8,128)(2,1)S(1)} collective-permute-done((bf16[2,256,384]{2,1,0:T(8,128)(2,1)S(1)}, bf16[2,256,384]{2,1,0:T(8,128)(2,1)S(1)}, u32[]{:S(2)}, u32[]{:S(2)}) %collective-permute-start.11) | collective-permute-done | bytes 393248 | tf_op jit(solution)/shard_map/ppermute | solution.py:32
  44.2 2.2 %shard_map.47.refs_3_ = f32[256,1152]{1,0:T(8,128)S(1)} custom-call(bf16[4,256,384]{2,1,0:T(8,128)(2,1)S(1)} %collective-permute-done.4.refs_0_, bf16[4,256,384]{2,1,0:T(8,128)(2,1)S(1)} %collective-permute-done.5.refs_1_, bf16[6144,1152]{1,0:T(8,128)(2,1)S(1)} %shard_map.39.refs_4_.refs_1_.refs_2_, f32[256,1152]{1,0:T(8,128)S(1)} %shard_map.42.refs_2_.refs_3_, ...), custom_call_target="tpu_custom_call" | custom-call | flops 1 | bytes 1 | tf_op jit(solution)/shard_map/pallas_call | solution.py:71
  49.7 2.2 %collective-permute-done.16.refs_0_ = bf16[256,384]{1,0:T(8,128)(2,1)S(1)} collective-permute-done((bf16[256,384]{1,0:T(8,128)(2,1)S(1)}, bf16[256,384]{1,0:T(8,128)(2,1)S(1)}, u32[]{:S(2)}, u32[]{:S(2)}) %collective-permute-start.16) | collective-permute-done | bytes 196640 | tf_op jit(solution)/shard_map/ppermute | solution.py:37
  51.8 1.8 %collective-permute-start.17 = (bf16[256,384]{1,0:T(8,128)(2,1)S(1)}, bf16[256,384]{1,0:T(8,128)(2,1)S(1)}, u32[]{:S(2)}, u32[]{:S(2)}) collective-permute-start(bf16[256,384]{1,0:T(8,128)(2,1)S(1)} %collective-permute-done.16.refs_0_), channel_id=1, source_target_pairs={{0,1},{1,2},{2,3},{3,0},{4,5},{5,6},{6,7},{7,4},{8,9},{9,10},{10,1... | collective-permute-start | bytes 589832 | tf_op jit(solution)/shard_map/ppermute | solution.py:32
  57.1 1.5 %collective-permute-start.13 = (bf16[256,384]{1,0:T(8,128)(2,1)S(1)}, bf16[256,384]{1,0:T(8,128)(2,1)S(1)}, u32[]{:S(2)}, u32[]{:S(2)}) collective-permute-start(bf16[256,384]{1,0:T(8,128)(2,1)S(1)} %collective-permute-done.12.refs_4_.refs_0_), channel_id=1, source_target_pairs={{0,1},{1,2},{2,3},{3,0},{4,5},{5,6},{6,7},{7,4},{8,9},{9,10},{10,1... | collective-permute-start | bytes 589832 | tf_op jit(solution)/shard_map/ppermute | solution.py:32
  58.6 1.8 %collective-permute-start.14 = (bf16[256,384]{1,0:T(8,128)(2,1)S(1)}, bf16[256,384]{1,0:T(8,128)(2,1)S(1)}, u32[]{:S(2)}, u32[]{:S(2)}) collective-permute-start(bf16[256,384]{1,0:T(8,128)(2,1)S(1)} %collective-permute-done.12.refs_4_.refs_0_), channel_id=1, source_target_pairs={{0,3},{1,0},{2,1},{3,2},{4,7},{5,4},{6,5},{7,6},{8,11},{9,8},{10,9... | collective-permute-start | bytes 589832 | tf_op jit(solution)/shard_map/ppermute | solution.py:32
  63.1 1.6 %collective-permute-start.23 = (bf16[4,256,384]{2,1,0:T(8,128)(2,1)S(1)}, bf16[4,256,384]{2,1,0:T(8,128)(2,1)S(1)}, u32[]{:S(2)}, u32[]{:S(2)}) collective-permute-start(bf16[4,256,384]{2,1,0:T(8,128)(2,1)S(1)} %shard_map.49.refs_4_.refs_0_), channel_id=1, source_target_pairs={{0,12},{1,13},{2,14},{3,15},{4,0},{5,1},{6,2},{7,3},{8,4},{9,5},{1... | collective-permute-start | bytes 2359304 | tf_op jit(solution)/shard_map/ppermute | solution.py:32
  64.7 1.6 %collective-permute-done.13.refs_1_ = bf16[256,384]{1,0:T(8,128)(2,1)S(1)} collective-permute-done((bf16[256,384]{1,0:T(8,128)(2,1)S(1)}, bf16[256,384]{1,0:T(8,128)(2,1)S(1)}, u32[]{:S(2)}, u32[]{:S(2)}) %collective-permute-start.13) | collective-permute-done | bytes 196640 | tf_op jit(solution)/shard_map/ppermute | solution.py:32
  66.4 3.8 %collective-permute-done.15.refs_3_ = bf16[256,384]{1,0:T(8,128)(2,1)S(1)} collective-permute-done((bf16[256,384]{1,0:T(8,128)(2,1)S(1)}, bf16[256,384]{1,0:T(8,128)(2,1)S(1)}, u32[]{:S(2)}, u32[]{:S(2)}) %collective-permute-start.15) | collective-permute-done | bytes 196640 | tf_op jit(solution)/shard_map/ppermute | solution.py:32
  70.3 2.0 %collective-permute-start.21 = (bf16[4,256,384]{2,1,0:T(8,128)(2,1)S(1)}, bf16[4,256,384]{2,1,0:T(8,128)(2,1)S(1)}, u32[]{:S(2)}, u32[]{:S(2)}) collective-permute-start(bf16[4,256,384]{2,1,0:T(8,128)(2,1)S(1)} %shard_map.50.refs_2_.refs_0_.refs_4_), channel_id=1, source_target_pairs={{0,12},{1,13},{2,14},{3,15},{4,0},{5,1},{6,2},{7,3},{8,4},{9,5},{1... | collective-permute-start | bytes 2359304 | tf_op jit(solution)/shard_map/ppermute | solution.py:32
  74.7 1.6 %collective-permute-done.23.refs_1_ = bf16[4,256,384]{2,1,0:T(8,128)(2,1)S(1)} collective-permute-done((bf16[4,256,384]{2,1,0:T(8,128)(2,1)S(1)}, bf16[4,256,384]{2,1,0:T(8,128)(2,1)S(1)}, u32[]{:S(2)}, u32[]{:S(2)}) %collective-permute-start.23) | collective-permute-done | bytes 786464 | tf_op jit(solution)/shard_map/ppermute | solution.py:32
  76.8 1.7 %collective-permute-start.27 = (bf16[2,256,384]{2,1,0:T(8,128)(2,1)S(1)}, bf16[2,256,384]{2,1,0:T(8,128)(2,1)S(1)}, u32[]{:S(2)}, u32[]{:S(2)}) collective-permute-start(bf16[2,256,384]{2,1,0:T(8,128)(2,1)S(1)} %get-tuple-element.24), channel_id=1, source_target_pairs={{0,12},{1,13},{2,14},{3,15},{4,0},{5,1},{6,2},{7,3},{8,4},{9,5},{1... | collective-permute-start | bytes 1179656 | tf_op jit(solution)/shard_map/ppermute | solution.py:32
  78.5 2.2 %shard_map.54.refs_2_.refs_3_ = f32[256,1152]{1,0:T(8,128)S(1)} custom-call(bf16[4,256,384]{2,1,0:T(8,128)(2,1)S(1)} %collective-permute-done.22.refs_0_, bf16[4,256,384]{2,1,0:T(8,128)(2,1)S(1)} %collective-permute-done.23.refs_1_, bf16[6144,1152]{1,0:T(8,128)(2,1)S(1)} %shard_map.39.refs_4_.refs_1_.refs_2_, f32[256,1152]{1,0:T(8,128)S(1)} %shard_map.51.refs_2_.refs_3_, ...), custom_call_target="tpu_custom_call" | custom-call | flops 1 | bytes 1 | tf_op jit(solution)/shard_map/pallas_call | solution.py:71
  80.7 2.4 %collective-permute-done.20.refs_0_ = bf16[4,256,384]{2,1,0:T(8,128)(2,1)S(1)} collective-permute-done((bf16[4,256,384]{2,1,0:T(8,128)(2,1)S(1)}, bf16[4,256,384]{2,1,0:T(8,128)(2,1)S(1)}, u32[]{:S(2)}, u32[]{:S(2)}) %collective-permute-start.20) | collective-permute-done | bytes 786464 | tf_op jit(solution)/shard_map/ppermute | solution.py:32
  83.1 1.7 %collective-permute-done.21.refs_1_ = bf16[4,256,384]{2,1,0:T(8,128)(2,1)S(1)} collective-permute-done((bf16[4,256,384]{2,1,0:T(8,128)(2,1)S(1)}, bf16[4,256,384]{2,1,0:T(8,128)(2,1)S(1)}, u32[]{:S(2)}, u32[]{:S(2)}) %collective-permute-start.21) | collective-permute-done | bytes 786464 | tf_op jit(solution)/shard_map/ppermute | solution.py:32
  85.2 1.7 %collective-permute-start.25 = (bf16[2,256,384]{2,1,0:T(8,128)(2,1)S(1)}, bf16[2,256,384]{2,1,0:T(8,128)(2,1)S(1)}, u32[]{:S(2)}, u32[]{:S(2)}) collective-permute-start(bf16[2,256,384]{2,1,0:T(8,128)(2,1)S(1)} %get-tuple-element.23), channel_id=1, source_target_pairs={{0,12},{1,13},{2,14},{3,15},{4,0},{5,1},{6,2},{7,3},{8,4},{9,5},{1... | collective-permute-start | bytes 1179656 | tf_op jit(solution)/shard_map/ppermute | solution.py:32
  87.3 1.7 %collective-permute-done.27.refs_1_ = bf16[2,256,384]{2,1,0:T(8,128)(2,1)S(1)} collective-permute-done((bf16[2,256,384]{2,1,0:T(8,128)(2,1)S(1)}, bf16[2,256,384]{2,1,0:T(8,128)(2,1)S(1)}, u32[]{:S(2)}, u32[]{:S(2)}) %collective-permute-start.27) | collective-permute-done | bytes 393248 | tf_op jit(solution)/shard_map/ppermute | solution.py:32
  90.2 2.2 %shard_map.57.refs_3_ = f32[256,1152]{1,0:T(8,128)S(1)} custom-call(bf16[4,256,384]{2,1,0:T(8,128)(2,1)S(1)} %collective-permute-done.20.refs_0_, bf16[4,256,384]{2,1,0:T(8,128)(2,1)S(1)} %collective-permute-done.21.refs_1_, bf16[6144,1152]{1,0:T(8,128)(2,1)S(1)} %shard_map.39.refs_4_.refs_1_.refs_2_, f32[256,1152]{1,0:T(8,128)S(1)} %shard_map.52.refs_2_.refs_3_, ...), custom_call_target="tpu_custom_call" | custom-call | flops 1 | bytes 1 | tf_op jit(solution)/shard_map/pallas_call | solution.py:71
  92.7 1.5 %collective-permute-done.25.refs_1_ = bf16[2,256,384]{2,1,0:T(8,128)(2,1)S(1)} collective-permute-done((bf16[2,256,384]{2,1,0:T(8,128)(2,1)S(1)}, bf16[2,256,384]{2,1,0:T(8,128)(2,1)S(1)}, u32[]{:S(2)}, u32[]{:S(2)}) %collective-permute-start.25) | collective-permute-done | bytes 393248 | tf_op jit(solution)/shard_map/ppermute | solution.py:32
  94.2 1.9 %shard_map.58 = bf16[512,384]{1,0:T(8,128)(2,1)} custom-call(bf16[2,256,384]{2,1,0:T(8,128)(2,1)S(1)} %collective-permute-done.24.refs_0_, bf16[2,256,384]{2,1,0:T(8,128)(2,1)S(1)} %collective-permute-done.25.refs_1_, bf16[6144,1152]{1,0:T(8,128)(2,1)S(1)} %shard_map.39.refs_4_.refs_1_.refs_2_, f32[256,1152]{1,0:T(8,128)S(1)} %shard_map.57.refs_3_, ...), custom_call_target="tpu_custom_call" | custom-call | flops 1 | bytes 1 | tf_op jit(solution)/shard_map/pallas_call | solution.py:71
  (46 shorter events, 22.9 us)
Async XLA Ops:
  0.0 17.0 %collective-permute-start.3 = (bf16[3,3072,384]{2,1,0:T(8,128)(2,1)}, bf16[3,3072,384]{2,1,0:T(8,128)(2,1)S(1)}, u32[]{:S(2)}, u32[]{:S(2)}) collective-permute-start(bf16[3,3072,384]{2,1,0:T(8,128)(2,1)} %bitcast.4), channel_id=1, source_target_pairs={{0,16},{16,0},{1,17},{17,1},{2,18},{18,2},{3,19},{19,3},{4,20},{20... | collective-permute-start | bytes 21233672 | tf_op jit(solution)/shard_map/ppermute | solution.py:258
  1.1 9.5 %collective-permute-start.2 = (bf16[512,384]{1,0:T(8,128)(2,1)S(1)}, bf16[512,384]{1,0:T(8,128)(2,1)S(1)}, u32[]{:S(2)}, u32[]{:S(2)}) collective-permute-start(bf16[512,384]{1,0:T(8,128)(2,1)S(1)} %get-tuple-element.15.refs_0_), channel_id=1, source_target_pairs={{0,2},{1,3},{2,0},{3,1},{4,6},{5,7},{6,4},{7,5},{8,10},{9,11},{10,... | collective-permute-start | bytes 1179656 | tf_op jit(solution)/shard_map/ppermute | solution.py:32
  4.3 10.5 %collective-permute-start = (bf16[512,384]{1,0:T(8,128)(2,1)}, bf16[512,384]{1,0:T(8,128)(2,1)S(1)}, u32[]{:S(2)}, u32[]{:S(2)}) collective-permute-start(bf16[512,384]{1,0:T(8,128)(2,1)} %bitcast.8), channel_id=1, source_target_pairs={{0,1},{1,2},{2,3},{3,0},{4,5},{5,6},{6,7},{7,4},{8,9},{9,10},{10,1... | collective-permute-start | bytes 1179656 | tf_op jit(solution)/shard_map/ppermute | solution.py:32
  4.8 10.0 %collective-permute-start.1 = (bf16[512,384]{1,0:T(8,128)(2,1)}, bf16[512,384]{1,0:T(8,128)(2,1)S(1)}, u32[]{:S(2)}, u32[]{:S(2)}) collective-permute-start(bf16[512,384]{1,0:T(8,128)(2,1)} %bitcast.9), channel_id=1, source_target_pairs={{0,3},{1,0},{2,1},{3,2},{4,7},{5,4},{6,5},{7,6},{8,11},{9,8},{10,9... | collective-permute-start | bytes 1179656 | tf_op jit(solution)/shard_map/ppermute | solution.py:32
  14.9 12.1 %collective-permute-start.6 = (bf16[4,256,384]{2,1,0:T(8,128)(2,1)S(1)}, bf16[4,256,384]{2,1,0:T(8,128)(2,1)S(1)}, u32[]{:S(2)}, u32[]{:S(2)}) collective-permute-start(bf16[4,256,384]{2,1,0:T(8,128)(2,1)S(1)} %shard_map.38.refs_2_.refs_0_.refs_4_), channel_id=1, source_target_pairs={{0,4},{1,5},{2,6},{3,7},{4,8},{5,9},{6,10},{7,11},{8,12},{9,13},{1... | collective-permute-start | bytes 2359304 | tf_op jit(solution)/shard_map/ppermute | solution.py:32
  16.8 13.2 %collective-permute-start.7 = (bf16[4,256,384]{2,1,0:T(8,128)(2,1)S(1)}, bf16[4,256,384]{2,1,0:T(8,128)(2,1)S(1)}, u32[]{:S(2)}, u32[]{:S(2)}) collective-permute-start(bf16[4,256,384]{2,1,0:T(8,128)(2,1)S(1)} %shard_map.38.refs_2_.refs_0_.refs_4_), channel_id=1, source_target_pairs={{0,12},{1,13},{2,14},{3,15},{4,0},{5,1},{6,2},{7,3},{8,4},{9,5},{1... | collective-permute-start | bytes 2359304 | tf_op jit(solution)/shard_map/ppermute | solution.py:32
  21.4 14.0 %collective-permute-start.4 = (bf16[4,256,384]{2,1,0:T(8,128)(2,1)S(1)}, bf16[4,256,384]{2,1,0:T(8,128)(2,1)S(1)}, u32[]{:S(2)}, u32[]{:S(2)}) collective-permute-start(bf16[4,256,384]{2,1,0:T(8,128)(2,1)S(1)} %shard_map.40.refs_2_.refs_0_.refs_4_), channel_id=1, source_target_pairs={{0,4},{1,5},{2,6},{3,7},{4,8},{5,9},{6,10},{7,11},{8,12},{9,13},{1... | collective-permute-start | bytes 2359304 | tf_op jit(solution)/shard_map/ppermute | solution.py:32
  23.8 14.7 %collective-permute-start.5 = (bf16[4,256,384]{2,1,0:T(8,128)(2,1)S(1)}, bf16[4,256,384]{2,1,0:T(8,128)(2,1)S(1)}, u32[]{:S(2)}, u32[]{:S(2)}) collective-permute-start(bf16[4,256,384]{2,1,0:T(8,128)(2,1)S(1)} %shard_map.40.refs_2_.refs_0_.refs_4_), channel_id=1, source_target_pairs={{0,12},{1,13},{2,14},{3,15},{4,0},{5,1},{6,2},{7,3},{8,4},{9,5},{1... | collective-permute-start | bytes 2359304 | tf_op jit(solution)/shard_map/ppermute | solution.py:32
  30.1 10.5 %collective-permute-start.10 = (bf16[2,256,384]{2,1,0:T(8,128)(2,1)S(1)}, bf16[2,256,384]{2,1,0:T(8,128)(2,1)S(1)}, u32[]{:S(2)}, u32[]{:S(2)}) collective-permute-start(bf16[2,256,384]{2,1,0:T(8,128)(2,1)S(1)} %get-tuple-element.16.refs_4_), channel_id=1, source_target_pairs={{0,4},{1,5},{2,6},{3,7},{4,8},{5,9},{6,10},{7,11},{8,12},{9,13},{1... | collective-permute-start | bytes 1179656 | tf_op jit(solution)/shard_map/ppermute | solution.py:32
  30.2 12.5 %collective-permute-start.11 = (bf16[2,256,384]{2,1,0:T(8,128)(2,1)S(1)}, bf16[2,256,384]{2,1,0:T(8,128)(2,1)S(1)}, u32[]{:S(2)}, u32[]{:S(2)}) collective-permute-start(bf16[2,256,384]{2,1,0:T(8,128)(2,1)S(1)} %get-tuple-element.19), channel_id=1, source_target_pairs={{0,12},{1,13},{2,14},{3,15},{4,0},{5,1},{6,2},{7,3},{8,4},{9,5},{1... | collective-permute-start | bytes 1179656 | tf_op jit(solution)/shard_map/ppermute | solution.py:32
  38.5 7.9 %collective-permute-start.8 = (bf16[2,256,384]{2,1,0:T(8,128)(2,1)S(1)}, bf16[2,256,384]{2,1,0:T(8,128)(2,1)S(1)}, u32[]{:S(2)}, u32[]{:S(2)}) collective-permute-start(bf16[2,256,384]{2,1,0:T(8,128)(2,1)S(1)} %get-tuple-element.17.refs_6_), channel_id=1, source_target_pairs={{0,4},{1,5},{2,6},{3,7},{4,8},{5,9},{6,10},{7,11},{8,12},{9,13},{1... | collective-permute-start | bytes 1179656 | tf_op jit(solution)/shard_map/ppermute | solution.py:32
  38.6 9.1 %collective-permute-start.9 = (bf16[2,256,384]{2,1,0:T(8,128)(2,1)S(1)}, bf16[2,256,384]{2,1,0:T(8,128)(2,1)S(1)}, u32[]{:S(2)}, u32[]{:S(2)}) collective-permute-start(bf16[2,256,384]{2,1,0:T(8,128)(2,1)S(1)} %get-tuple-element.18), channel_id=1, source_target_pairs={{0,12},{1,13},{2,14},{3,15},{4,0},{5,1},{6,2},{7,3},{8,4},{9,5},{1... | collective-permute-start | bytes 1179656 | tf_op jit(solution)/shard_map/ppermute | solution.py:32
  43.9 7.9 %collective-permute-start.16 = (bf16[256,384]{1,0:T(8,128)(2,1)S(1)}, bf16[256,384]{1,0:T(8,128)(2,1)S(1)}, u32[]{:S(2)}, u32[]{:S(2)}) collective-permute-start(bf16[256,384]{1,0:T(8,128)(2,1)S(1)} %shard_map.46.refs_4_), channel_id=1, source_target_pairs={{0,32},{32,64},{64,96},{96,128},{128,160},{160,192},{192,224},{224... | collective-permute-start | bytes 589832 | tf_op jit(solution)/shard_map/ppermute | solution.py:37
  48.9 8.2 %collective-permute-start.12 = (bf16[256,384]{1,0:T(8,128)(2,1)S(1)}, bf16[256,384]{1,0:T(8,128)(2,1)S(1)}, u32[]{:S(2)}, u32[]{:S(2)}) collective-permute-start(bf16[256,384]{1,0:T(8,128)(2,1)S(1)} %shard_map.48), channel_id=1, source_target_pairs={{0,32},{32,64},{64,96},{96,128},{128,160},{160,192},{192,224},{224... | collective-permute-start | bytes 589832 | tf_op jit(solution)/shard_map/ppermute | solution.py:37
  51.8 8.5 %collective-permute-start.17 = (bf16[256,384]{1,0:T(8,128)(2,1)S(1)}, bf16[256,384]{1,0:T(8,128)(2,1)S(1)}, u32[]{:S(2)}, u32[]{:S(2)}) collective-permute-start(bf16[256,384]{1,0:T(8,128)(2,1)S(1)} %collective-permute-done.16.refs_0_), channel_id=1, source_target_pairs={{0,1},{1,2},{2,3},{3,0},{4,5},{5,6},{6,7},{7,4},{8,9},{9,10},{10,1... | collective-permute-start | bytes 589832 | tf_op jit(solution)/shard_map/ppermute | solution.py:32
  53.6 7.8 %collective-permute-start.18 = (bf16[256,384]{1,0:T(8,128)(2,1)S(1)}, bf16[256,384]{1,0:T(8,128)(2,1)S(1)}, u32[]{:S(2)}, u32[]{:S(2)}) collective-permute-start(bf16[256,384]{1,0:T(8,128)(2,1)S(1)} %collective-permute-done.16.refs_0_), channel_id=1, source_target_pairs={{0,3},{1,0},{2,1},{3,2},{4,7},{5,4},{6,5},{7,6},{8,11},{9,8},{10,9... | collective-permute-start | bytes 589832 | tf_op jit(solution)/shard_map/ppermute | solution.py:32
  55.1 7.2 %collective-permute-start.19 = (bf16[256,384]{1,0:T(8,128)(2,1)S(1)}, bf16[256,384]{1,0:T(8,128)(2,1)S(1)}, u32[]{:S(2)}, u32[]{:S(2)}) collective-permute-start(bf16[256,384]{1,0:T(8,128)(2,1)S(1)} %collective-permute-done.16.refs_0_), channel_id=1, source_target_pairs={{0,2},{1,3},{2,0},{3,1},{4,6},{5,7},{6,4},{7,5},{8,10},{9,11},{10,... | collective-permute-start | bytes 589832 | tf_op jit(solution)/shard_map/ppermute | solution.py:32
  57.1 9.1 %collective-permute-start.13 = (bf16[256,384]{1,0:T(8,128)(2,1)S(1)}, bf16[256,384]{1,0:T(8,128)(2,1)S(1)}, u32[]{:S(2)}, u32[]{:S(2)}) collective-permute-start(bf16[256,384]{1,0:T(8,128)(2,1)S(1)} %collective-permute-done.12.refs_4_.refs_0_), channel_id=1, source_target_pairs={{0,1},{1,2},{2,3},{3,0},{4,5},{5,6},{6,7},{7,4},{8,9},{9,10},{10,1... | collective-permute-start | bytes 589832 | tf_op jit(solution)/shard_map/ppermute | solution.py:32
  58.6 7.8 %collective-permute-start.14 = (bf16[256,384]{1,0:T(8,128)(2,1)S(1)}, bf16[256,384]{1,0:T(8,128)(2,1)S(1)}, u32[]{:S(2)}, u32[]{:S(2)}) collective-permute-start(bf16[256,384]{1,0:T(8,128)(2,1)S(1)} %collective-permute-done.12.refs_4_.refs_0_), channel_id=1, source_target_pairs={{0,3},{1,0},{2,1},{3,2},{4,7},{5,4},{6,5},{7,6},{8,11},{9,8},{10,9... | collective-permute-start | bytes 589832 | tf_op jit(solution)/shard_map/ppermute | solution.py:32
  60.4 9.8 %collective-permute-start.15 = (bf16[256,384]{1,0:T(8,128)(2,1)S(1)}, bf16[256,384]{1,0:T(8,128)(2,1)S(1)}, u32[]{:S(2)}, u32[]{:S(2)}) collective-permute-start(bf16[256,384]{1,0:T(8,128)(2,1)S(1)} %collective-permute-done.12.refs_4_.refs_0_), channel_id=1, source_target_pairs={{0,2},{1,3},{2,0},{3,1},{4,6},{5,7},{6,4},{7,5},{8,10},{9,11},{10,... | collective-permute-start | bytes 589832 | tf_op jit(solution)/shard_map/ppermute | solution.py:32
  62.4 12.3 %collective-permute-start.22 = (bf16[4,256,384]{2,1,0:T(8,128)(2,1)S(1)}, bf16[4,256,384]{2,1,0:T(8,128)(2,1)S(1)}, u32[]{:S(2)}, u32[]{:S(2)}) collective-permute-start(bf16[4,256,384]{2,1,0:T(8,128)(2,1)S(1)} %shard_map.49.refs_4_.refs_0_), channel_id=1, source_target_pairs={{0,4},{1,5},{2,6},{3,7},{4,8},{5,9},{6,10},{7,11},{8,12},{9,13},{1... | collective-permute-start | bytes 2359304 | tf_op jit(solution)/shard_map/ppermute | solution.py:32
  63.1 13.2 %collective-permute-start.23 = (bf16[4,256,384]{2,1,0:T(8,128)(2,1)S(1)}, bf16[4,256,384]{2,1,0:T(8,128)(2,1)S(1)}, u32[]{:S(2)}, u32[]{:S(2)}) collective-permute-start(bf16[4,256,384]{2,1,0:T(8,128)(2,1)S(1)} %shard_map.49.refs_4_.refs_0_), channel_id=1, source_target_pairs={{0,12},{1,13},{2,14},{3,15},{4,0},{5,1},{6,2},{7,3},{8,4},{9,5},{1... | collective-permute-start | bytes 2359304 | tf_op jit(solution)/shard_map/ppermute | solution.py:32
  70.2 12.9 %collective-permute-start.20 = (bf16[4,256,384]{2,1,0:T(8,128)(2,1)S(1)}, bf16[4,256,384]{2,1,0:T(8,128)(2,1)S(1)}, u32[]{:S(2)}, u32[]{:S(2)}) collective-permute-start(bf16[4,256,384]{2,1,0:T(8,128)(2,1)S(1)} %shard_map.50.refs_2_.refs_0_.refs_4_), channel_id=1, source_target_pairs={{0,4},{1,5},{2,6},{3,7},{4,8},{5,9},{6,10},{7,11},{8,12},{9,13},{1... | collective-permute-start | bytes 2359304 | tf_op jit(solution)/shard_map/ppermute | solution.py:32
  70.3 14.4 %collective-permute-start.21 = (bf16[4,256,384]{2,1,0:T(8,128)(2,1)S(1)}, bf16[4,256,384]{2,1,0:T(8,128)(2,1)S(1)}, u32[]{:S(2)}, u32[]{:S(2)}) collective-permute-start(bf16[4,256,384]{2,1,0:T(8,128)(2,1)S(1)} %shard_map.50.refs_2_.refs_0_.refs_4_), channel_id=1, source_target_pairs={{0,12},{1,13},{2,14},{3,15},{4,0},{5,1},{6,2},{7,3},{8,4},{9,5},{1... | collective-permute-start | bytes 2359304 | tf_op jit(solution)/shard_map/ppermute | solution.py:32
  76.4 10.9 %collective-permute-start.26 = (bf16[2,256,384]{2,1,0:T(8,128)(2,1)S(1)}, bf16[2,256,384]{2,1,0:T(8,128)(2,1)S(1)}, u32[]{:S(2)}, u32[]{:S(2)}) collective-permute-start(bf16[2,256,384]{2,1,0:T(8,128)(2,1)S(1)} %get-tuple-element.21.refs_4_), channel_id=1, source_target_pairs={{0,4},{1,5},{2,6},{3,7},{4,8},{5,9},{6,10},{7,11},{8,12},{9,13},{1... | collective-permute-start | bytes 1179656 | tf_op jit(solution)/shard_map/ppermute | solution.py:32
  76.8 12.2 %collective-permute-start.27 = (bf16[2,256,384]{2,1,0:T(8,128)(2,1)S(1)}, bf16[2,256,384]{2,1,0:T(8,128)(2,1)S(1)}, u32[]{:S(2)}, u32[]{:S(2)}) collective-permute-start(bf16[2,256,384]{2,1,0:T(8,128)(2,1)S(1)} %get-tuple-element.24), channel_id=1, source_target_pairs={{0,12},{1,13},{2,14},{3,15},{4,0},{5,1},{6,2},{7,3},{8,4},{9,5},{1... | collective-permute-start | bytes 1179656 | tf_op jit(solution)/shard_map/ppermute | solution.py:32
  84.8 7.9 %collective-permute-start.24 = (bf16[2,256,384]{2,1,0:T(8,128)(2,1)S(1)}, bf16[2,256,384]{2,1,0:T(8,128)(2,1)S(1)}, u32[]{:S(2)}, u32[]{:S(2)}) collective-permute-start(bf16[2,256,384]{2,1,0:T(8,128)(2,1)S(1)} %get-tuple-element.22.refs_5_), channel_id=1, source_target_pairs={{0,4},{1,5},{2,6},{3,7},{4,8},{5,9},{6,10},{7,11},{8,12},{9,13},{1... | collective-permute-start | bytes 1179656 | tf_op jit(solution)/shard_map/ppermute | solution.py:32
  85.2 9.0 %collective-permute-start.25 = (bf16[2,256,384]{2,1,0:T(8,128)(2,1)S(1)}, bf16[2,256,384]{2,1,0:T(8,128)(2,1)S(1)}, u32[]{:S(2)}, u32[]{:S(2)}) collective-permute-start(bf16[2,256,384]{2,1,0:T(8,128)(2,1)S(1)} %get-tuple-element.23), channel_id=1, source_target_pairs={{0,12},{1,13},{2,14},{3,15},{4,0},{5,1},{6,2},{7,3},{8,4},{9,5},{1... | collective-permute-start | bytes 1179656 | tf_op jit(solution)/shard_map/ppermute | solution.py:32
